TPU v7x, 512 devices: a whole 4x4x16 slice. The times are simulated.
512 devices in a mesh: seq: 32 (over z, core), help: 16 (over y, x).
Axes of the slice: x: 4, y: 4, z: 16, core: 2. Of those that a mesh axis runs over, the one named last changes fastest.
Arguments:
- queries: bfloat16 [2560, 64, 640], P(('seq', 'help')), may hold values from -6 to 6
- key_rows: bfloat16 [2560, 64, 640], P(('seq', 'help')), may hold values from -6 to 6
- value_rows: bfloat16 [2560, 64, 640], P(('seq', 'help')), may hold values from -6 to 6
- grad_out: bfloat16 [2560, 64, 1280], P(('seq', 'help')), may hold values from -24 to 24
- proj_weight: bfloat16 [640, 1280], P('seq'), may hold values from -0.25 to 0.25
- proj_bias: bfloat16 [1280], P('seq'), may hold values from -3 to 3
- live_count: int32 [512], P(('seq', 'help')), may hold values from 1 to 5, as said below
Outputs:
- encoded: bfloat16 [2560, 64, 1280], P(('seq', 'help'))
- grad_queries: bfloat16 [2560, 64, 640], P(('seq', 'help'))
- grad_keys: bfloat16 [2560, 64, 640], P(('seq', 'help'))
- grad_values: bfloat16 [2560, 64, 640], P(('seq', 'help'))
- weight_grad: float32 [640, 1280], P('seq')
- bias_grad: float32 [1280], P('seq')
Inputs may be any that keep to these rules, and one draw needn't show every extreme that they name: Device d's first live_count[d] slots hold image windows, its other slots are empty; some device holds 5.
All inputs are finite; a program needn't handle non-finite values.
Results may differ from a plain program's by a relative error of at most 0.04.
Values may be sent and summed in bfloat16 or wider, within the bound.
No kernel may reach another device: no remote copies, remote signals or barrier semaphores. Data moves between devices by JAX's collectives and lax.ppermute only.
A program may use at most 64 MiB of HBM per device.

v0:
```python
import jax
import jax.numpy as jnp
from jax import lax
from jax.sharding import PartitionSpec as P

H = 8
HD = 80


def window_pass(query_win, key_win, value_win, grad_win, full_weight, full_bias):
    scale = HD ** (-0.5)
    tokens = query_win.shape[0]
    query_heads = query_win.reshape(tokens, H, HD)
    key_heads = key_win.reshape(tokens, H, HD)
    value_heads = value_win.reshape(tokens, H, HD)
    scores = (
        jnp.einsum("qhd,khd->hqk", query_heads, key_heads, preferred_element_type=jnp.float32)
        * scale
    )
    probs = jax.nn.softmax(scores, axis=-1)
    probs_low = probs.astype(jnp.bfloat16)
    attended = jnp.einsum(
        "hqk,khd->qhd", probs_low, value_heads, preferred_element_type=jnp.float32
    )
    attended = attended.reshape(tokens, H * HD).astype(jnp.bfloat16)
    encoded = (
        jnp.dot(attended, full_weight, preferred_element_type=jnp.float32)
        + full_bias.astype(jnp.float32)
    ).astype(jnp.bfloat16)
    grad_attended = lax.dot_general(
        grad_win, full_weight, (((1,), (1,)), ((), ())), preferred_element_type=jnp.float32
    ).astype(jnp.bfloat16)
    grad_heads = grad_attended.reshape(tokens, H, HD)
    attended_heads = attended.reshape(tokens, H, HD)
    grad_values = jnp.einsum(
        "hqk,qhd->khd", probs_low, grad_heads, preferred_element_type=jnp.float32
    )
    delta = jnp.einsum(
        "qhd,qhd->hq", grad_heads, attended_heads, preferred_element_type=jnp.float32
    )
    grad_probs = jnp.einsum(
        "qhd,khd->hqk", grad_heads, value_heads, preferred_element_type=jnp.float32
    )
    grad_scores = (probs * (grad_probs - delta[:, :, None])).astype(jnp.bfloat16)
    grad_queries = (
        jnp.einsum("hqk,khd->qhd", grad_scores, key_heads, preferred_element_type=jnp.float32)
        * scale
    )
    grad_keys = (
        jnp.einsum("hqk,qhd->khd", grad_scores, query_heads, preferred_element_type=jnp.float32)
        * scale
    )
    weight_term = lax.dot_general(
        attended, grad_win, (((0,), (0,)), ((), ())), preferred_element_type=jnp.float32
    )
    bias_term = jnp.sum(grad_win.astype(jnp.float32), axis=0)
    return (
        encoded,
        grad_queries.reshape(tokens, H * HD).astype(jnp.bfloat16),
        grad_keys.reshape(tokens, H * HD).astype(jnp.bfloat16),
        grad_values.reshape(tokens, H * HD).astype(jnp.bfloat16),
        weight_term,
        bias_term,
    )


def run_slots(sources, upper, results, weight_sum, bias_sum, full_weight, full_bias, place):

    def visit(step_index, carry):
        results, weight_sum, bias_sum = carry
        slot = place(step_index)
        pieces = [lax.dynamic_index_in_dim(source, slot, 0, keepdims=False) for source in sources]
        made = window_pass(pieces[0], pieces[1], pieces[2], pieces[3], full_weight, full_bias)
        results = tuple(
            (
                lax.dynamic_update_index_in_dim(whole, made_part, slot, 0)
                for whole, made_part in zip(results, made[:4])
            )
        )
        return (results, weight_sum + made[4], bias_sum + made[5])

    return lax.fori_loop(0, upper, visit, (results, weight_sum, bias_sum))


def same_slot(step_index):
    return step_index


def on_device(queries, key_rows, value_rows, grad_out, proj_weight, proj_bias, live_count):
    full_weight, full_bias = (
        lax.all_gather(proj_weight, "seq", axis=0, tiled=True),
        lax.all_gather(proj_bias, "seq", axis=0, tiled=True),
    )
    count = live_count[0]
    sources = (queries, key_rows, value_rows, grad_out)
    results = (
        jnp.zeros_like(grad_out),
        jnp.zeros_like(queries),
        jnp.zeros_like(queries),
        jnp.zeros_like(queries),
    )
    weight_sum = jnp.zeros(full_weight.shape, jnp.float32)
    bias_sum = jnp.zeros(full_bias.shape, jnp.float32)
    results, weight_sum, bias_sum = run_slots(
        sources, count, results, weight_sum, bias_sum, full_weight, full_bias, same_slot
    )
    total_weight, total_bias = lax.psum((weight_sum, bias_sum), ("seq", "help"))
    position = lax.axis_index("seq")
    weight_grad = lax.dynamic_slice_in_dim(
        total_weight, position * proj_weight.shape[0], proj_weight.shape[0], 0
    )
    bias_grad = lax.dynamic_slice_in_dim(
        total_bias, position * proj_bias.shape[0], proj_bias.shape[0], 0
    )
    encoded, grad_queries, grad_keys, grad_values = results
    return (encoded, grad_queries, grad_keys, grad_values, weight_grad, bias_grad)


def solution(mesh):
    placed = (
        P(("seq", "help"), None, None),
        P(("seq", "help"), None, None),
        P(("seq", "help"), None, None),
        P(("seq", "help"), None, None),
        P("seq", None),
        P("seq"),
        P(("seq", "help")),
    )
    return jax.shard_map(
        on_device,
        mesh=mesh,
        in_specs=placed,
        out_specs=(
            P(("seq", "help"), None, None),
            P(("seq", "help"), None, None),
            P(("seq", "help"), None, None),
            P(("seq", "help"), None, None),
            P("seq", None),
            P("seq"),
        ),
        check_vma=False,
    )
```

profile of v0, /device:TPU:1, one launch (start us, length us, event | category | flops | bytes accessed | tf_op | source)
XLA Modules:
  0.0 665.8 jit_solution(6612862615343161436)
XLA Ops:
  7.2 0.0 all-gather.3.cloned.1.call-start
  7.2 0.7 all-gather.3.cloned.1.call-update
  7.9 0.0 all-reduce.3.cloned.1.call-start
  8.0 1.3 dynamic-slice
  9.9 0.9 dynamic-update-slice
  10.7 54.2 %all-reduce = bf16[1280]{0:T(1024)(128)(2,1)S(1)} all-reduce(bf16[1280]{0:T(1024)(128)(2,1)S(1)} %dynamic-update-slice), channel_id=1, replica_groups=mesh['seq'=32,'help'=16] {'seq'}, use_global_device_ids=true, to_apply=%add | all-reduce | flops 1280 | bytes 5120
  64.9 22.6 %all-gather.3.cloned.1.call-done = bf16[32,20,1280]{2,1,0:T(8,128)(2,1)} async-done(((bf16[1,20,1280]{2,1,0:T(8,128)(2,1)}), bf16[32,20,1280]{2,1,0:T(8,128)(2,1)}) %all-gather.3.cloned.1.call-update) | async-done | bytes 1638416 | tf_op jit(solution)/shard_map/all_gather | solution.py:91
  87.5 2.5 reshape.77
  90.0 0.0 copy-start
  90.0 0.9 broadcast_in_dim.21
  91.0 0.8 broadcast.16
  91.7 0.8 broadcast.16.clone
  92.5 0.8 broadcast.16.clone.1
  93.3 1.9 broadcast_in_dim.22
  95.3 0.0 copy-done
  95.3 16.4 %while.20 = (s32[]{:T(128)}, bf16[5,64,1280]{2,1,0:T(8,128)(2,1)}, bf16[5,64,640]{2,1,0:T(8,128)(2,1)}, bf16[5,64,640]{2,1,0:T(8,128)(2,1)}, bf16[5,64,640]{2,1,...) while((s32[]{:T(128)}, bf16[5,64,1280]{2,1,0:T(8,128)(2,1)}, ...), condition=%wide.region_4.5_spmd, body=%wide.region_0.4_spmd.sunk | while | flops 358606784 | bytes 15905515 | solution.py:82
  95.9 0.6 convolution_convert_fusion.4
  96.5 0.2 reshape.87
  96.7 0.9 constant_dynamic-slice_fusion.7
  97.6 0.2 reshape.88
  97.8 0.9 constant_dynamic-slice_fusion.8
  98.7 0.2 reshape.89
  98.9 0.9 fusion.117
  99.8 0.9 constant_dynamic-slice_fusion.9
  100.7 0.2 reshape.90
  100.9 0.5 multiply_reduce_fusion.2
  101.4 0.1 copy.138
  101.5 0.1 convert_element_type.128
  101.6 1.0 fusion.118
  102.7 1.1 fusion.119
  103.8 0.2 fusion.120
  104.1 0.1 copy.139
  104.2 0.1 convert_element_type.130
  104.3 0.6 constant_dynamic-update-slice_fusion.5
  105.0 0.4 fusion.121
  105.3 0.1 copy.140
  105.4 0.1 convert_element_type.131
  105.6 0.2 fusion.122
  105.7 0.1 copy.141
  105.8 0.1 convert_element_type.132
  106.0 0.7 constant_dynamic-update-slice_fusion.6
  106.7 4.3 convolution_add_fusion.3
  111.6 0.0 all-reduce.3.cloned.1.call-update
  111.7 165.2 %psum.15 = f32[1280]{0:T(1024)S(1)} all-reduce(f32[1280]{0:T(1024)S(1)} %get-tuple-element.89), channel_id=1, replica_groups=mesh['seq'=32,'help'=16] {'seq','help'}, use_global_device_ids=true, to_apply=%region_6.7 | all-reduce | flops 1280 | bytes 10240 | tf_op jit(solution)/shard_map/psum | solution.py:107
  276.8 0.6 dynamic_slice.21
  277.4 380.0 %all-reduce.3.cloned.1.call-done = f32[640,1280]{1,0:T(8,128)} async-done(((f32[640,1280]{1,0:T(8,128)}), f32[640,1280]{1,0:T(8,128)}) %all-reduce.3.cloned.1.call-update) | async-done | bytes 3276816 | tf_op jit(solution)/shard_map/psum | solution.py:107
  657.4 1.6 constant_dynamic-slice_fusion.3
  (6 shorter events, 0.1 us)
Async XLA Ops:
  7.2 80.4 %all-gather.3.cloned.1.call-start = ((), (), s32[]{:S(2)}) async-start(), calls=%async_computation.1 | async-start | bytes 2027520 | tf_op jit(solution)/shard_map/all_gather | solution.py:91
  7.9 649.5 %all-reduce.3.cloned.1.call-start = ((), (), s32[]{:S(2)}) async-start(), calls=%async_computation | async-start | bytes 6553600 | tf_op jit(solution)/shard_map/psum | solution.py:107
  90.0 5.2 copy-start
Sparse Core Ops, SparseCore 0:
  10.1 77.3 all-gather.2
  111.8 545.5 all-reduce.2
where the time goes:
time: 667 us; the launch traced here: 666 us
  waiting for transfers between devices  403 us (60%)
  blocking collectives  219 us (33%)
  local copies, waits for them, and re-layouts  17.6 us (3%)
  between operations  14.7 us (2%)
  matrix products  9.27 us (1%)
    psum x1, waiting for transfers between devices, on_device(): total_weight, total_bias = lax.psum((weight_sum, bias_sum), ('seq', 'help'))  380 us
    psum x1, blocking collectives, on_device(): total_weight, total_bias = lax.psum((weight_sum, bias_sum), ('seq', 'help'))  165 us
    unnamed x1, blocking collectives  54.2 us
    all_gather x1, waiting for transfers between devices, on_device(): lax.all_gather(proj_weight, 'seq', axis=0, tiled=True)  22.6 us
  transfers between devices with their start and end apart: 2, of which 2 were waited for; matrix products, arithmetic and copies ran while one was open for 0% of the time, Pallas kernels for 0%

commit v1 on v0

v1 whole, which is shorter than its diff:
```python
import jax
import jax.numpy as jnp
from jax import lax
from jax.experimental import pallas as pl
from jax.experimental.pallas import tpu as pltpu
from jax.sharding import Mesh
from jax.sharding import PartitionSpec as P

H = 8
HD = 80
WIN = 64
CAP = 5
ATTN = 640
D = 1280
Z, CORES, Y, X = 16, 2, 4, 4
SEQ = Z * CORES
HELP = Y * X
ROWS = ATTN // SEQ
BIAS = D // SEQ
BLOCKS = D // 128
PAIRS = H // 2
SPAN = 256
PART = 13
UNITS = HELP * PART
SCALE = HD**-0.5
VMEM_LIMIT = 60 * 1024 * 1024
NT = (((1,), (1,)), ((), ()))
TN = (((0,), (0,)), ((), ()))
NN = (((1,), (0,)), ((), ()))


def mm(left, right, dims):
    return lax.dot_general(left, right, dims, preferred_element_type=jnp.float32)


def head_masks(pair):
    lane = lax.broadcasted_iota(jnp.int32, (1, SPAN), 1)
    first = 32 * pair
    in_a = (lane >= first) & (lane < first + HD)
    in_b = (lane >= first + HD) & (lane < first + 2 * HD)
    return in_a.astype(jnp.float32), in_b.astype(jnp.float32)


def stacked(rows, mask_a, mask_b):
    return jnp.concatenate(
        [rows * mask_a.astype(jnp.bfloat16), rows * mask_b.astype(jnp.bfloat16)], axis=0
    )


def add_span(tiles, pair, value):
    for part in range(2):
        piece = value[:, 128 * part : 128 * (part + 1)]
        at = pair + part
        tiles[at] = piece if tiles[at] is None else tiles[at] + piece


def bias_pick():
    from_place = lax.broadcasted_iota(jnp.int32, (D, 128), 0)
    to_lane = lax.broadcasted_iota(jnp.int32, (D, 128), 1)
    return jnp.where(lax.rem(from_place, BIAS) == to_lane, 1.0, 0.0).astype(jnp.bfloat16)


def bias_owner(core):
    seq = lax.broadcasted_iota(jnp.int32, (Z, D), 0) * CORES + core
    place = lax.broadcasted_iota(jnp.int32, (Z, D), 1)
    return (place >= seq * BIAS) & (place < (seq + 1) * BIAS)


def forward_kernel(
    count_ref, core_ref, q_hbm, k_hbm, v_hbm, g_hbm, probs_hbm, att_hbm, own_hbm, other_hbm,
    q_ref, k_ref, v_ref, g_ref, probs_ref, att_ref, own_ref, other_ref, acc,
    in_sems, g_sem, out_sems, wire_sems,
):
    count, my_core = count_ref[0], core_ref[0]
    masks = [head_masks(pair) for pair in range(PAIRS)]
    moves = [
        [
            pltpu.make_async_copy(far.at[w], near.at[w], in_sems.at[which, w])
            for which, (far, near) in enumerate(((q_hbm, q_ref), (k_hbm, k_ref), (v_hbm, v_ref)))
        ]
        for w in range(CAP)
    ]
    for window_moves in moves:
        for move in window_moves:
            move.start()
    g_move = pltpu.make_async_copy(g_hbm, g_ref, g_sem)
    g_move.start()
    back = []
    for w in range(CAP):
        for move in moves[w]:
            move.wait()
        rows = slice(WIN * w, WIN * (w + 1))
        tiles = [None] * (PAIRS + 1)
        for pair in range(PAIRS):
            span = slice(128 * pair, 128 * pair + SPAN)
            mask_a, mask_b = masks[pair]
            q_both = stacked(q_ref[w, :, span], mask_a, mask_b)
            scores = mm(k_ref[w, :, span], q_both, NT) * SCALE
            raised = jnp.exp(scores - jnp.max(scores, axis=0, keepdims=True))
            probs = raised / jnp.sum(raised, axis=0, keepdims=True)
            probs_ref[w, :, 128 * pair : 128 * (pair + 1)] = probs
            both = mm(probs.astype(jnp.bfloat16), v_ref[w, :, span], TN)
            add_span(tiles, pair, both[:WIN] * mask_a + both[WIN:] * mask_b)
        keep = jnp.where(w < count, 1.0, 0.0)
        for at, tile in enumerate(tiles):
            att_ref[rows, 128 * at : 128 * (at + 1)] = (tile * keep).astype(jnp.bfloat16)
        back.append(pltpu.make_async_copy(probs_ref.at[w], probs_hbm.at[w], out_sems.at[0, w]))
        back[-1].start()
        back.append(
            pltpu.make_async_copy(
                att_ref.at[pl.ds(WIN * w, WIN)],
                att_hbm.at[pl.ds(WIN * w, WIN)],
                out_sems.at[1, w],
            )
        )
        back[-1].start()
    row_of = lax.broadcasted_iota(jnp.int32, (16, CAP * WIN), 1)
    live_rows = jnp.where(row_of < count * WIN, 1.0, 0.0).astype(jnp.bfloat16)
    left = jnp.concatenate([att_ref[...].T, live_rows], axis=0)
    g_move.wait()
    bias_parts = []
    for block in range(0, BLOCKS, 2):
        made = mm(left, g_ref[:, 128 * block : 128 * (block + 2)], NN)
        acc[block] = made[:ATTN, :128]
        acc[block + 1] = made[:ATTN, 128:]
        bias_parts.append(made[ATTN : ATTN + 1])
    bias_row = jnp.concatenate(bias_parts, axis=1)
    pick = bias_pick()
    for which, (core, wire_ref, wire_hbm) in enumerate(
        ((1 - my_core, other_ref, other_hbm), (my_core, own_ref, own_hbm))
    ):
        for row in range(ROWS):
            for block in range(BLOCKS):
                wire_ref[row * BLOCKS + block] = acc[
                    block, pl.ds(core * ROWS + row, Z, stride=CORES * ROWS), :
                ].astype(jnp.bfloat16)
        owned = jnp.where(bias_owner(core), jnp.broadcast_to(bias_row, (Z, D)), 0.0)
        wire_ref[ROWS * BLOCKS] = mm(owned.astype(jnp.bfloat16), pick, NN).astype(jnp.bfloat16)
        for unit in range(ROWS * BLOCKS + 1, UNITS):
            wire_ref[unit] = jnp.zeros((Z, 128), jnp.bfloat16)
        back.append(pltpu.make_async_copy(wire_ref, wire_hbm, wire_sems.at[which]))
        back[-1].start()
    for move in back:
        move.wait()


def backward_kernel(
    count_ref, core_ref, q_hbm, k_hbm, v_hbm, g_hbm, probs_hbm, att_hbm, near_hbm, far_hbm,
    enc_hbm, dq_hbm, dk_hbm, dv_hbm,
    q_ref, k_ref, v_ref, g_ref, probs_ref, att_ref, near_ref, far_ref,
    enc_ref, dq_ref, dk_ref, dv_ref,
    grad_att, wide, weight_ref, in_sems, out_sems, enc_sem,
):
    count, my_core = count_ref[0], core_ref[0]
    moves = [
        pltpu.make_async_copy(there, here, in_sems.at[at])
        for at, (there, here) in enumerate(
            (
                (near_hbm, near_ref), (far_hbm, far_ref), (att_hbm, att_ref), (g_hbm, g_ref),
                (v_hbm, v_ref), (probs_hbm, probs_ref), (q_hbm, q_ref), (k_hbm, k_ref),
            )
        )
    ]
    for move in moves:
        move.start()
    masks = [head_masks(pair) for pair in range(PAIRS)]
    bias_pieces = []
    for which, (held, core) in enumerate(((near_ref, my_core), (far_ref, 1 - my_core))):
        moves[which].wait()
        for unit in range(ROWS * BLOCKS + 1):
            owner, at = divmod(unit, PART)
            piece = held[owner, at]
            row, block = divmod(unit, BLOCKS)
            if row < ROWS:
                wide[block, pl.ds(core * ROWS + row, Z, stride=CORES * ROWS), :] = piece.astype(
                    jnp.float32
                )
            else:
                spread = mm(piece, bias_pick(), NT)
                bias_pieces.append(jnp.where(bias_owner(core), spread, 0.0))
    bias = jnp.sum(bias_pieces[0] + bias_pieces[1], axis=0, keepdims=True)
    for block in range(BLOCKS):
        weight_ref[:, 128 * block : 128 * (block + 1)] = wide[block].astype(jnp.bfloat16)
    moves[2].wait()
    live_rows = lax.broadcasted_iota(jnp.int32, (CAP * WIN, 1), 0) < count * WIN
    for block in range(0, BLOCKS, 2):
        cols = slice(128 * block, 128 * (block + 2))
        encoded = mm(att_ref[...], weight_ref[:, cols], NN) + bias[:, cols]
        encoded = jnp.where(live_rows, encoded, 0.0).astype(jnp.bfloat16)
        for w in range(CAP):
            enc_ref[w, :, cols] = encoded[WIN * w : WIN * (w + 1)]
    back = [pltpu.make_async_copy(enc_ref, enc_hbm, enc_sem)]
    back[0].start()
    for move in moves[3:]:
        move.wait()
    grad_att[...] = mm(g_ref[...], weight_ref[...], NT).astype(jnp.bfloat16)
    results = ((dq_ref, dq_hbm), (dk_ref, dk_hbm), (dv_ref, dv_hbm))
    for w in range(CAP):
        rows = slice(WIN * w, WIN * (w + 1))
        keep = jnp.where(w < count, 1.0, 0.0)
        dq_tiles, dk_tiles, dv_tiles = ([None] * (PAIRS + 1) for _ in range(3))
        for pair in range(PAIRS):
            span = slice(128 * pair, 128 * pair + SPAN)
            mask_a, mask_b = masks[pair]
            g_both = stacked(grad_att[rows, span], mask_a, mask_b)
            q_both = stacked(q_ref[w, :, span], mask_a, mask_b)
            grad_probs = mm(v_ref[w, :, span], g_both, NT)
            probs = probs_ref[w, :, 128 * pair : 128 * (pair + 1)]
            probs_low = probs.astype(jnp.bfloat16)
            delta = jnp.sum(probs_low.astype(jnp.float32) * grad_probs, axis=0, keepdims=True)
            grad_scores = (probs * (grad_probs - delta)).astype(jnp.bfloat16)
            add_span(dv_tiles, pair, mm(probs_low, g_both, NN))
            add_span(dk_tiles, pair, mm(grad_scores, q_both, NN))
            both = mm(grad_scores, k_ref[w, :, span], TN)
            add_span(dq_tiles, pair, both[:WIN] * mask_a + both[WIN:] * mask_b)
        for at in range(PAIRS + 1):
            cols = slice(128 * at, 128 * (at + 1))
            dq_ref[w, :, cols] = (dq_tiles[at] * (keep * SCALE)).astype(jnp.bfloat16)
            dk_ref[w, :, cols] = (dk_tiles[at] * (keep * SCALE)).astype(jnp.bfloat16)
            dv_ref[w, :, cols] = (dv_tiles[at] * keep).astype(jnp.bfloat16)
        for which, (made, out) in enumerate(results):
            move = pltpu.make_async_copy(made.at[w], out.at[w], out_sems.at[which, w])
            move.start()
            back.append(move)
    for move in back:
        move.wait()


def hbm_spec():
    return pl.BlockSpec(memory_space=pltpu.HBM)


def smem_spec():
    return pl.BlockSpec(memory_space=pltpu.SMEM)


def forward(count, core, queries, key_rows, value_rows, grads):
    return pl.pallas_call(
        forward_kernel,
        out_shape=(
            jax.ShapeDtypeStruct((CAP, WIN, H * WIN), jnp.float32),
            jax.ShapeDtypeStruct((CAP * WIN, ATTN), jnp.bfloat16),
            jax.ShapeDtypeStruct((UNITS, Z, 128), jnp.bfloat16),
            jax.ShapeDtypeStruct((UNITS, Z, 128), jnp.bfloat16),
        ),
        in_specs=[smem_spec()] * 2 + [hbm_spec()] * 4,
        out_specs=(hbm_spec(),) * 4,
        scratch_shapes=[
            pltpu.VMEM((CAP, WIN, ATTN), jnp.bfloat16),
            pltpu.VMEM((CAP, WIN, ATTN), jnp.bfloat16),
            pltpu.VMEM((CAP, WIN, ATTN), jnp.bfloat16),
            pltpu.VMEM((CAP * WIN, D), jnp.bfloat16),
            pltpu.VMEM((CAP, WIN, H * WIN), jnp.float32),
            pltpu.VMEM((CAP * WIN, ATTN), jnp.bfloat16),
            pltpu.VMEM((UNITS, Z, 128), jnp.bfloat16),
            pltpu.VMEM((UNITS, Z, 128), jnp.bfloat16),
            pltpu.VMEM((BLOCKS, ATTN, 128), jnp.float32),
            pltpu.SemaphoreType.DMA((3, CAP)),
            pltpu.SemaphoreType.DMA,
            pltpu.SemaphoreType.DMA((2, CAP)),
            pltpu.SemaphoreType.DMA((2,)),
        ],
        compiler_params=pltpu.CompilerParams(vmem_limit_bytes=VMEM_LIMIT),
        cost_estimate=pl.CostEstimate(
            flops=800_000_000, bytes_accessed=5_000_000, transcendentals=200_000
        ),
    )(count, core, queries, key_rows, value_rows, grads)


def backward(count, core, queries, key_rows, value_rows, grads, probs, attended, near, far):
    rows = jax.ShapeDtypeStruct((CAP, WIN, ATTN), jnp.bfloat16)
    return pl.pallas_call(
        backward_kernel,
        out_shape=(jax.ShapeDtypeStruct((CAP, WIN, D), jnp.bfloat16), rows, rows, rows),
        in_specs=[smem_spec()] * 2 + [hbm_spec()] * 8,
        out_specs=(hbm_spec(),) * 4,
        scratch_shapes=[
            pltpu.VMEM((CAP, WIN, ATTN), jnp.bfloat16),
            pltpu.VMEM((CAP, WIN, ATTN), jnp.bfloat16),
            pltpu.VMEM((CAP, WIN, ATTN), jnp.bfloat16),
            pltpu.VMEM((CAP * WIN, D), jnp.bfloat16),
            pltpu.VMEM((CAP, WIN, H * WIN), jnp.float32),
            pltpu.VMEM((CAP * WIN, ATTN), jnp.bfloat16),
            pltpu.VMEM((HELP, PART + 2, Z, 128), jnp.bfloat16),
            pltpu.VMEM((HELP, PART + 2, Z, 128), jnp.bfloat16),
            pltpu.VMEM((CAP, WIN, D), jnp.bfloat16),
            pltpu.VMEM((CAP, WIN, ATTN), jnp.bfloat16),
            pltpu.VMEM((CAP, WIN, ATTN), jnp.bfloat16),
            pltpu.VMEM((CAP, WIN, ATTN), jnp.bfloat16),
            pltpu.VMEM((CAP * WIN, ATTN), jnp.bfloat16),
            pltpu.VMEM((BLOCKS, ATTN, 128), jnp.float32),
            pltpu.VMEM((ATTN, D), jnp.bfloat16),
            pltpu.SemaphoreType.DMA((8,)),
            pltpu.SemaphoreType.DMA((3, CAP)),
            pltpu.SemaphoreType.DMA,
        ],
        compiler_params=pltpu.CompilerParams(vmem_limit_bytes=VMEM_LIMIT),
        cost_estimate=pl.CostEstimate(
            flops=1_500_000_000, bytes_accessed=8_000_000, transcendentals=0
        ),
    )(count, core, queries, key_rows, value_rows, grads, probs, attended, near, far)


def exchange(blocks, axis):
    return lax.all_to_all(blocks, axis, 0, 0, tiled=True)


def other_core(value):
    return lax.ppermute(value, "c", [(0, 1), (1, 0)])


def added(parts):
    return jnp.sum(parts.astype(jnp.float32), axis=0)


def own_units(proj_weight, proj_bias):
    units = jnp.concatenate(
        [
            proj_weight.reshape(ROWS * BLOCKS, 128),
            jnp.pad(proj_bias, (0, 128 - BIAS))[None],
            jnp.zeros((UNITS - ROWS * BLOCKS - 1, 128), jnp.bfloat16),
        ],
        axis=0,
    )
    mine = lax.axis_index("y") * X + lax.axis_index("x")
    return lax.dynamic_index_in_dim(units.reshape(HELP, PART, 128), mine, 0, keepdims=False)


def on_device(queries, key_rows, value_rows, grad_out, proj_weight, proj_bias, live_count):
    core = lax.axis_index("c").reshape(1)
    grads = grad_out.reshape(CAP * WIN, D)
    share = own_units(proj_weight, proj_bias)
    probs, attended, own, other = forward(live_count, core, queries, key_rows, value_rows, grads)
    both = added(jnp.stack([own, other_core(other)])).astype(jnp.bfloat16)
    over_help = exchange(both.reshape(HELP, PART, Z, 128), ("y", "x"))
    part = added(over_help).astype(jnp.bfloat16).transpose(1, 0, 2)
    shares = jnp.broadcast_to(share[None], (Z, PART, 128))
    over_z = exchange(jnp.concatenate([part, shares], axis=1), "z")
    whole = added(over_z[:, :PART])
    high = whole.astype(jnp.bfloat16)
    low = (whole - high.astype(jnp.float32)).astype(jnp.bfloat16)
    ends = jnp.pad(jnp.stack([high, low]), ((0, 0), (0, Z - PART), (0, 0)))
    sent = jnp.concatenate([over_z[:, PART:].transpose(1, 0, 2), ends], axis=0)
    near = exchange(jnp.broadcast_to(sent[None], (HELP, PART + 2, Z, 128)), ("y", "x"))
    encoded, grad_queries, grad_keys, grad_values = backward(
        live_count, core, queries, key_rows, value_rows, grads, probs, attended, near,
        other_core(near),
    )
    units = near[:, PART, :PART].astype(jnp.float32) + near[:, PART + 1, :PART].astype(jnp.float32)
    units = units.reshape(UNITS, 128)
    weight_grad = units[: ROWS * BLOCKS].reshape(ROWS, D)
    bias_grad = units[ROWS * BLOCKS, :BIAS]
    return (encoded, grad_queries, grad_keys, grad_values, weight_grad, bias_grad)


def solution(mesh):
    torus = Mesh(mesh.devices.reshape(Z, CORES, Y, X), ("z", "c", "y", "x"))
    windows = P(("z", "c", "y", "x"), None, None)
    lines, line = P(("z", "c"), None), P(("z", "c"))
    return jax.shard_map(
        on_device,
        mesh=torus,
        in_specs=(windows, windows, windows, windows, lines, line, P(("z", "c", "y", "x"))),
        out_specs=(windows, windows, windows, windows, lines, line),
        check_vma=False,
    )
```

time: 667 us -> 99.7 us (0.15)
  waiting for transfers between devices: 403 us -> 16.6 us
  blocking collectives: 219 us -> 40.5 us
  starting transfers between devices: 0.08 us -> 19.2 us
  Pallas kernels: 0 us -> 15.5 us
  local copies, waits for them, and re-layouts: 17.6 us -> 3.21 us
  between operations: 14.7 us -> 1.48 us
  matrix products: 9.27 us -> 0 us
    psum x1 -> x0, waiting for transfers between devices: 380 us -> none  [on_device(): total_weight, total_bias = lax.psum((weight_sum, bias_sum), ('seq', 'help'))]
    psum x1 -> x0, blocking collectives: 165 us -> none  [on_device(): total_weight, total_bias = lax.psum((weight_sum, bias_sum), ('seq', 'help'))]
    unnamed x1 -> x0, blocking collectives: 54.2 us -> none
    all_to_all x0 -> x2, blocking collectives: none -> 40.5 us  [exchange(): return lax.all_to_all(blocks, axis, 0, 0, tiled=True)]
    all_gather x1 -> x0, waiting for transfers between devices: 22.6 us -> none  [on_device(): lax.all_gather(proj_weight, 'seq', axis=0, tiled=True)]
    pallas_call x0 -> x2, Pallas kernels: none -> 15.5 us  [the longest x1 8.77 us: backward(): pl.pallas_call(backward_kernel, out_shape=(jax.ShapeDtypeStruct((CAP, WIN...]
    ppermute x0 -> x2, starting transfers between devices: none -> 15.5 us  [other_core(): return lax.ppermute(value, 'c', [(0, 1), (1, 0)])]
    all_to_all x0 -> x1, waiting for transfers between devices: none -> 13.5 us  [exchange(): return lax.all_to_all(blocks, axis, 0, 0, tiled=True)]
  transfers between devices with their start and end apart: 2 -> 3, of which waited for: 2 -> 3; matrix products, arithmetic and copies ran while one was open for 0% -> 2% of each run, Pallas kernels for 0% -> 0%
where the time goes in v1:
time: 99.7 us; the launch traced here: 99.2 us
  blocking collectives  40.5 us (41%)
  starting transfers between devices  19.2 us (19%)
  waiting for transfers between devices  16.6 us (17%)
  Pallas kernels  15.5 us (16%)
  local copies, waits for them, and re-layouts  3.21 us (3%)
  other arithmetic  2.63 us (3%)
  between operations  1.48 us (1%)
    all_to_all x2, blocking collectives, exchange(): return lax.all_to_all(blocks, axis, 0, 0, tiled=True)  40.5 us
    ppermute x2, starting transfers between devices, other_core(): return lax.ppermute(value, 'c', [(0, 1), (1, 0)])  15.5 us
    all_to_all x1, waiting for transfers between devices, exchange(): return lax.all_to_all(blocks, axis, 0, 0, tiled=True)  13.5 us
    pallas_call x1, Pallas kernels, backward(): pl.pallas_call(backward_kernel, out_shape=(jax.ShapeDtypeStruct((CAP, WIN...  8.77 us
    pallas_call x1, Pallas kernels, forward(): pl.pallas_call(forward_kernel, out_shape=(jax.ShapeDtypeStruct((CAP, WIN,...  6.78 us
    all_to_all x1, starting transfers between devices, exchange(): return lax.all_to_all(blocks, axis, 0, 0, tiled=True)  3.75 us
    ppermute x2, waiting for transfers between devices, other_core(): return lax.ppermute(value, 'c', [(0, 1), (1, 0)])  3.13 us
    reduce_sum x3, other arithmetic, added(): return jnp.sum(parts.astype(jnp.float32), axis=0)  2.45 us
  transfers between devices with their start and end apart: 3, of which 3 were waited for; matrix products, arithmetic and copies ran while one was open for 2% of the time, Pallas kernels for 0%

profile of v1, /device:TPU:1, one launch (start us, length us, event | category | flops | bytes accessed | tf_op | source)
XLA Modules:
  0.0 99.2 jit_solution(16678592442229763303)
XLA Ops:
  1.3 6.8 %shard_map.118 = (f32[5,64,512]{2,1,0:T(8,128)}, bf16[320,640]{1,0:T(8,128)(2,1)}, bf16[208,16,128]{2,1,0:T(8,128)(2,1)}, bf16[208,16,128]{2,1,0:T(8,128)(2,1)}) custom-call(s32[1]{0:T(128)S(6)} %copy.16.count_ref, s32[1]{0:T(128)} %bitcast.core_ref, bf16[5,64,640]{2,1,0:T(8,128)(2,1)} %q_hbm.3, bf16[5,64,640]{2,1,0:T(8,128)(2,1)} %k_hbm.3, ...), custom_call_target="tpu_custom_call" | custom-call | flops 800000000 | bytes 5000000 | tf_op jit(solution)/shard_map/pallas_call | solution.py:238
  8.1 8.8 %collective-permute-start = (bf16[208,16,128]{2,1,0:T(8,128)(2,1)}, bf16[208,16,128]{2,1,0:T(8,128)(2,1)S(1)}, u32[]{:S(2)}, u32[]{:S(2)}) collective-permute-start(bf16[208,16,128]{2,1,0:T(8,128)(2,1)} %get-tuple-element.17), channel_id=1, source_target_pairs={{0,16},{16,0},{1,17},{17,1},{2,18},{18,2},{3,19},{19,3},{4,20},{20... | collective-permute-start | bytes 2555912 | tf_op jit(solution)/shard_map/ppermute | solution.py:309
  16.9 2.2 %collective-permute-done = bf16[208,16,128]{2,1,0:T(8,128)(2,1)S(1)} collective-permute-done((bf16[208,16,128]{2,1,0:T(8,128)(2,1)}, bf16[208,16,128]{2,1,0:T(8,128)(2,1)S(1)}, u32[]{:S(2)}, u32[]{:S(2)}) %collective-permute-start) | collective-permute-done | bytes 852000 | tf_op jit(solution)/shard_map/ppermute | solution.py:309
  19.1 2.3 %reduce_sum.33 = bf16[208,16,128]{2,1,0:T(8,128)(2,1)} add(bf16[208,16,128]{2,1,0:T(8,128)(2,1)} %get-tuple-element.16, bf16[208,16,128]{2,1,0:T(8,128)(2,1)S(1)} %collective-permute-done) | non-fusion elementwise | flops 425984 | bytes 2555904 | tf_op jit(solution)/shard_map/reduce_sum | solution.py:313
  21.4 0.0 copy-start.1
  21.4 3.8 %all-to-all-start = ((bf16[16,13,16,128]{3,2,1,0:T(8,128)(2,1)}), bf16[16,13,16,128]{3,2,1,0:T(8,128)(2,1)S(1)}, u32[]{:S(2)}, u32[]{:S(2)}) async-start(bf16[16,13,16,128]{3,2,1,0:T(8,128)(2,1)} %bitcast.2), calls=%async_computation | async-start | bytes 1703936 | tf_op jit(solution)/shard_map/all_to_all | solution.py:305
  25.1 0.0 copy-done.1
  25.1 0.1 reshape.64
  25.3 0.0 copy-start.3
  25.3 0.1 pad.18.clone
  25.3 0.6 copy-done.3
  25.9 0.1 maximum_maximum_fusion
  26.1 13.5 %all-to-all-done = bf16[16,13,16,128]{3,2,1,0:T(8,128)(2,1)S(1)} async-done(((bf16[16,13,16,128]{3,2,1,0:T(8,128)(2,1)}), bf16[16,13,16,128]{3,2,1,0:T(8,128)(2,1)S(1)}, u32[]{:S(2)}, u32[]{:S(2)}) %all-to-all-start) | async-done | bytes 852000 | tf_op jit(solution)/shard_map/all_to_all | solution.py:305
  39.6 0.1 reduce_sum.34
  39.8 24.2 %all_to_all.15 = bf16[16,26,128]{2,1,0:T(8,128)(2,1)S(1)} all-to-all(bf16[16,26,128]{2,1,0:T(8,128)(2,1)S(1)} %copy.14), channel_id=1, replica_groups=mesh['z'=16,'c'=2,'y'=4,'x'=4] {'z'}, dimensions={0} | all-to-all | bytes 212992 | tf_op jit(solution)/shard_map/all_to_all | solution.py:305
  64.2 0.1 broadcast_in_dim.24
  64.3 16.3 %all_to_all.16.near_hbm = bf16[16,15,16,128]{3,2,1,0:T(8,128)(2,1)S(1)} all-to-all(bf16[16,15,16,128]{3,2,1,0:T(8,128)(2,1)S(1)} %broadcast_in_dim.24), channel_id=1, replica_groups=mesh['z'=16,'c'=2,'y'=4,'x'=4] {'y','x'}, dimensions={0} | all-to-all | bytes 1966080 | tf_op jit(solution)/shard_map/all_to_all | solution.py:305
  80.6 0.0 copy-start
  80.6 6.7 %collective-permute-start.1 = (bf16[16,15,16,128]{3,2,1,0:T(8,128)(2,1)S(1)}, bf16[16,15,16,128]{3,2,1,0:T(8,128)(2,1)S(1)}, u32[]{:S(2)}, u32[]{:S(2)}) collective-permute-start(bf16[16,15,16,128]{3,2,1,0:T(8,128)(2,1)S(1)} %all_to_all.16.near_hbm), channel_id=1, source_target_pairs={{0,16},{16,0},{1,17},{17,1},{2,18},{18,2},{3,19},{19,3},{4,20},{20... | collective-permute-start | bytes 2949128 | tf_op jit(solution)/shard_map/ppermute | solution.py:309
  87.4 0.7 reshape.66
  88.0 0.5 slice_bitcast_fusion.1
  88.5 0.9 collective-permute-done.1.far_hbm
  89.5 0.0 copy-start.2
  89.5 0.0 copy-done
  89.5 1.0 copy-done.2
  90.5 8.8 %shard_map.119 = (bf16[5,64,1280]{2,1,0:T(8,128)(2,1)}, bf16[5,64,640]{2,1,0:T(8,128)(2,1)}, bf16[5,64,640]{2,1,0:T(8,128)(2,1)}, bf16[5,64,640]{2,1,0:T(8,128)(2,1)}) custom-call(s32[1]{0:T(128)S(6)} %copy.16.count_ref, s32[1]{0:T(128)} %bitcast.core_ref, bf16[5,64,640]{2,1,0:T(8,128)(2,1)} %q_hbm.3, bf16[5,64,640]{2,1,0:T(8,128)(2,1)} %k_hbm.3, ...), custom_call_target="tpu_custom_call" | custom-call | flops 1500000000 | bytes 8000000 | tf_op jit(solution)/shard_map/pallas_call | solution.py:272
  (17 shorter events, 0.3 us)
Async XLA Ops:
  8.1 11.0 %collective-permute-start = (bf16[208,16,128]{2,1,0:T(8,128)(2,1)}, bf16[208,16,128]{2,1,0:T(8,128)(2,1)S(1)}, u32[]{:S(2)}, u32[]{:S(2)}) collective-permute-start(bf16[208,16,128]{2,1,0:T(8,128)(2,1)} %get-tuple-element.17), channel_id=1, source_target_pairs={{0,16},{16,0},{1,17},{17,1},{2,18},{18,2},{3,19},{19,3},{4,20},{20... | collective-permute-start | bytes 2555912 | tf_op jit(solution)/shard_map/ppermute | solution.py:309
  21.4 3.8 %copy-start.1 = (bf16[20,1280]{1,0:T(8,128)(2,1)S(1)}, bf16[20,1280]{1,0:T(8,128)(2,1)}, u32[]{:S(2)}) copy-start(bf16[20,1280]{1,0:T(8,128)(2,1)} %param.11) | copy-start | bytes 153604
  21.4 18.2 %all-to-all-start = ((bf16[16,13,16,128]{3,2,1,0:T(8,128)(2,1)}), bf16[16,13,16,128]{3,2,1,0:T(8,128)(2,1)S(1)}, u32[]{:S(2)}, u32[]{:S(2)}) async-start(bf16[16,13,16,128]{3,2,1,0:T(8,128)(2,1)} %bitcast.2), calls=%async_computation | async-start | bytes 1703936 | tf_op jit(solution)/shard_map/all_to_all | solution.py:305
  25.3 0.7 copy-start.3
  80.6 8.8 %copy-start = (bf16[16,15,16,128]{3,2,1,0:T(8,128)(2,1)}, bf16[16,15,16,128]{3,2,1,0:T(8,128)(2,1)S(1)}, u32[]{:S(2)}) copy-start(bf16[16,15,16,128]{3,2,1,0:T(8,128)(2,1)S(1)} %all_to_all.16.near_hbm) | copy-start | bytes 2949124
  80.6 8.8 %collective-permute-start.1 = (bf16[16,15,16,128]{3,2,1,0:T(8,128)(2,1)S(1)}, bf16[16,15,16,128]{3,2,1,0:T(8,128)(2,1)S(1)}, u32[]{:S(2)}, u32[]{:S(2)}) collective-permute-start(bf16[16,15,16,128]{3,2,1,0:T(8,128)(2,1)S(1)} %all_to_all.16.near_hbm), channel_id=1, source_target_pairs={{0,16},{16,0},{1,17},{17,1},{2,18},{18,2},{3,19},{19,3},{4,20},{20... | collective-permute-start | bytes 2949128 | tf_op jit(solution)/shard_map/ppermute | solution.py:309
  89.5 1.0 %copy-start.2 = (bf16[16,15,16,128]{3,2,1,0:T(8,128)(2,1)}, bf16[16,15,16,128]{3,2,1,0:T(8,128)(2,1)S(1)}, u32[]{:S(2)}) copy-start(bf16[16,15,16,128]{3,2,1,0:T(8,128)(2,1)S(1)} %collective-permute-done.1.far_hbm) | copy-start | bytes 2949124

commit v2 on v1

--- a/solution.py
+++ b/solution.py
@@ -23,7 +23,7 @@
 PART = 13
 UNITS = HELP * PART
 SCALE = HD**-0.5
-VMEM_LIMIT = 60 * 1024 * 1024
+VMEM_LIMIT = 24 * 1024 * 1024
 NT = (((1,), (1,)), ((), ()))
 TN = (((0,), (0,)), ((), ()))
 NN = (((1,), (0,)), ((), ()))
@@ -67,9 +67,8 @@
 
 
 def forward_kernel(
-    count_ref, core_ref, q_hbm, k_hbm, v_hbm, g_hbm, probs_hbm, att_hbm, own_hbm, other_hbm,
-    q_ref, k_ref, v_ref, g_ref, probs_ref, att_ref, own_ref, other_ref, acc,
-    in_sems, g_sem, out_sems, wire_sems,
+    count_ref, core_ref, q_hbm, k_hbm, v_hbm, g_hbm, probs_ref, att_ref, own_ref, other_ref,
+    q_ref, k_ref, v_ref, g_ref, acc, in_sems, g_sem,
 ):
     count, my_core = count_ref[0], core_ref[0]
     masks = [head_masks(pair) for pair in range(PAIRS)]
@@ -85,7 +84,6 @@
             move.start()
     g_move = pltpu.make_async_copy(g_hbm, g_ref, g_sem)
     g_move.start()
-    back = []
     for w in range(CAP):
         for move in moves[w]:
             move.wait()
@@ -104,16 +102,6 @@
         keep = jnp.where(w < count, 1.0, 0.0)
         for at, tile in enumerate(tiles):
             att_ref[rows, 128 * at : 128 * (at + 1)] = (tile * keep).astype(jnp.bfloat16)
-        back.append(pltpu.make_async_copy(probs_ref.at[w], probs_hbm.at[w], out_sems.at[0, w]))
-        back[-1].start()
-        back.append(
-            pltpu.make_async_copy(
-                att_ref.at[pl.ds(WIN * w, WIN)],
-                att_hbm.at[pl.ds(WIN * w, WIN)],
-                out_sems.at[1, w],
-            )
-        )
-        back[-1].start()
     row_of = lax.broadcasted_iota(jnp.int32, (16, CAP * WIN), 1)
     live_rows = jnp.where(row_of < count * WIN, 1.0, 0.0).astype(jnp.bfloat16)
     left = jnp.concatenate([att_ref[...].T, live_rows], axis=0)
@@ -126,9 +114,7 @@
         bias_parts.append(made[ATTN : ATTN + 1])
     bias_row = jnp.concatenate(bias_parts, axis=1)
     pick = bias_pick()
-    for which, (core, wire_ref, wire_hbm) in enumerate(
-        ((1 - my_core, other_ref, other_hbm), (my_core, own_ref, own_hbm))
-    ):
+    for core, wire_ref in ((my_core, own_ref), (1 - my_core, other_ref)):
         for row in range(ROWS):
             for block in range(BLOCKS):
                 wire_ref[row * BLOCKS + block] = acc[
@@ -138,35 +124,26 @@
         wire_ref[ROWS * BLOCKS] = mm(owned.astype(jnp.bfloat16), pick, NN).astype(jnp.bfloat16)
         for unit in range(ROWS * BLOCKS + 1, UNITS):
             wire_ref[unit] = jnp.zeros((Z, 128), jnp.bfloat16)
-        back.append(pltpu.make_async_copy(wire_ref, wire_hbm, wire_sems.at[which]))
-        back[-1].start()
-    for move in back:
-        move.wait()
 
 
 def backward_kernel(
-    count_ref, core_ref, q_hbm, k_hbm, v_hbm, g_hbm, probs_hbm, att_hbm, near_hbm, far_hbm,
+    count_ref, core_ref, q_hbm, k_hbm, v_hbm, g_hbm, probs_ref, att_ref, near_ref, far_ref,
     enc_hbm, dq_hbm, dk_hbm, dv_hbm,
-    q_ref, k_ref, v_ref, g_ref, probs_ref, att_ref, near_ref, far_ref,
-    enc_ref, dq_ref, dk_ref, dv_ref,
+    q_ref, k_ref, v_ref, g_ref, enc_ref, dq_ref, dk_ref, dv_ref,
     grad_att, wide, weight_ref, in_sems, out_sems, enc_sem,
 ):
     count, my_core = count_ref[0], core_ref[0]
     moves = [
         pltpu.make_async_copy(there, here, in_sems.at[at])
         for at, (there, here) in enumerate(
-            (
-                (near_hbm, near_ref), (far_hbm, far_ref), (att_hbm, att_ref), (g_hbm, g_ref),
-                (v_hbm, v_ref), (probs_hbm, probs_ref), (q_hbm, q_ref), (k_hbm, k_ref),
-            )
+            ((g_hbm, g_ref), (v_hbm, v_ref), (q_hbm, q_ref), (k_hbm, k_ref))
         )
     ]
     for move in moves:
         move.start()
     masks = [head_masks(pair) for pair in range(PAIRS)]
     bias_pieces = []
-    for which, (held, core) in enumerate(((near_ref, my_core), (far_ref, 1 - my_core))):
-        moves[which].wait()
+    for held, core in ((near_ref, my_core), (far_ref, 1 - my_core)):
         for unit in range(ROWS * BLOCKS + 1):
             owner, at = divmod(unit, PART)
             piece = held[owner, at]
@@ -181,7 +158,6 @@
     bias = jnp.sum(bias_pieces[0] + bias_pieces[1], axis=0, keepdims=True)
     for block in range(BLOCKS):
         weight_ref[:, 128 * block : 128 * (block + 1)] = wide[block].astype(jnp.bfloat16)
-    moves[2].wait()
     live_rows = lax.broadcasted_iota(jnp.int32, (CAP * WIN, 1), 0) < count * WIN
     for block in range(0, BLOCKS, 2):
         cols = slice(128 * block, 128 * (block + 2))
@@ -191,7 +167,7 @@
             enc_ref[w, :, cols] = encoded[WIN * w : WIN * (w + 1)]
     back = [pltpu.make_async_copy(enc_ref, enc_hbm, enc_sem)]
     back[0].start()
-    for move in moves[3:]:
+    for move in moves:
         move.wait()
     grad_att[...] = mm(g_ref[...], weight_ref[...], NT).astype(jnp.bfloat16)
     results = ((dq_ref, dq_hbm), (dk_ref, dk_hbm), (dv_ref, dv_hbm))
@@ -226,6 +202,18 @@
         move.wait()
 
 
+def in_hbm(value):
+    return pltpu.with_memory_space_constraint(value, pltpu.HBM)
+
+
+def in_vmem(value):
+    return pltpu.with_memory_space_constraint(value, pltpu.VMEM)
+
+
+def vmem_spec():
+    return pl.BlockSpec(memory_space=pltpu.VMEM)
+
+
 def hbm_spec():
     return pl.BlockSpec(memory_space=pltpu.HBM)
 
@@ -238,33 +226,27 @@
     return pl.pallas_call(
         forward_kernel,
         out_shape=(
-            jax.ShapeDtypeStruct((CAP, WIN, H * WIN), jnp.float32),
-            jax.ShapeDtypeStruct((CAP * WIN, ATTN), jnp.bfloat16),
-            jax.ShapeDtypeStruct((UNITS, Z, 128), jnp.bfloat16),
-            jax.ShapeDtypeStruct((UNITS, Z, 128), jnp.bfloat16),
-        ),
-        in_specs=[smem_spec()] * 2 + [hbm_spec()] * 4,
-        out_specs=(hbm_spec(),) * 4,
-        scratch_shapes=[
-            pltpu.VMEM((CAP, WIN, ATTN), jnp.bfloat16),
-            pltpu.VMEM((CAP, WIN, ATTN), jnp.bfloat16),
-            pltpu.VMEM((CAP, WIN, ATTN), jnp.bfloat16),
-            pltpu.VMEM((CAP * WIN, D), jnp.bfloat16),
             pltpu.VMEM((CAP, WIN, H * WIN), jnp.float32),
             pltpu.VMEM((CAP * WIN, ATTN), jnp.bfloat16),
             pltpu.VMEM((UNITS, Z, 128), jnp.bfloat16),
             pltpu.VMEM((UNITS, Z, 128), jnp.bfloat16),
+        ),
+        in_specs=[smem_spec()] * 2 + [hbm_spec()] * 4,
+        out_specs=(vmem_spec(),) * 4,
+        scratch_shapes=[
+            pltpu.VMEM((CAP, WIN, ATTN), jnp.bfloat16),
+            pltpu.VMEM((CAP, WIN, ATTN), jnp.bfloat16),
+            pltpu.VMEM((CAP, WIN, ATTN), jnp.bfloat16),
+            pltpu.VMEM((CAP * WIN, D), jnp.bfloat16),
             pltpu.VMEM((BLOCKS, ATTN, 128), jnp.float32),
             pltpu.SemaphoreType.DMA((3, CAP)),
             pltpu.SemaphoreType.DMA,
-            pltpu.SemaphoreType.DMA((2, CAP)),
-            pltpu.SemaphoreType.DMA((2,)),
         ],
         compiler_params=pltpu.CompilerParams(vmem_limit_bytes=VMEM_LIMIT),
         cost_estimate=pl.CostEstimate(
             flops=800_000_000, bytes_accessed=5_000_000, transcendentals=200_000
         ),
-    )(count, core, queries, key_rows, value_rows, grads)
+    )(count, core, *(in_hbm(array) for array in (queries, key_rows, value_rows, grads)))
 
 
 def backward(count, core, queries, key_rows, value_rows, grads, probs, attended, near, far):
@@ -272,17 +254,13 @@
     return pl.pallas_call(
         backward_kernel,
         out_shape=(jax.ShapeDtypeStruct((CAP, WIN, D), jnp.bfloat16), rows, rows, rows),
-        in_specs=[smem_spec()] * 2 + [hbm_spec()] * 8,
+        in_specs=[smem_spec()] * 2 + [hbm_spec()] * 4 + [vmem_spec()] * 4,
         out_specs=(hbm_spec(),) * 4,
         scratch_shapes=[
             pltpu.VMEM((CAP, WIN, ATTN), jnp.bfloat16),
             pltpu.VMEM((CAP, WIN, ATTN), jnp.bfloat16),
             pltpu.VMEM((CAP, WIN, ATTN), jnp.bfloat16),
             pltpu.VMEM((CAP * WIN, D), jnp.bfloat16),
-            pltpu.VMEM((CAP, WIN, H * WIN), jnp.float32),
-            pltpu.VMEM((CAP * WIN, ATTN), jnp.bfloat16),
-            pltpu.VMEM((HELP, PART + 2, Z, 128), jnp.bfloat16),
-            pltpu.VMEM((HELP, PART + 2, Z, 128), jnp.bfloat16),
             pltpu.VMEM((CAP, WIN, D), jnp.bfloat16),
             pltpu.VMEM((CAP, WIN, ATTN), jnp.bfloat16),
             pltpu.VMEM((CAP, WIN, ATTN), jnp.bfloat16),
@@ -290,7 +268,7 @@
             pltpu.VMEM((CAP * WIN, ATTN), jnp.bfloat16),
             pltpu.VMEM((BLOCKS, ATTN, 128), jnp.float32),
             pltpu.VMEM((ATTN, D), jnp.bfloat16),
-            pltpu.SemaphoreType.DMA((8,)),
+            pltpu.SemaphoreType.DMA((4,)),
             pltpu.SemaphoreType.DMA((3, CAP)),
             pltpu.SemaphoreType.DMA,
         ],
@@ -298,7 +276,10 @@
         cost_estimate=pl.CostEstimate(
             flops=1_500_000_000, bytes_accessed=8_000_000, transcendentals=0
         ),
-    )(count, core, queries, key_rows, value_rows, grads, probs, attended, near, far)
+    )(
+        count, core, *(in_hbm(array) for array in (queries, key_rows, value_rows, grads)),
+        *(in_vmem(array) for array in (probs, attended, near, far)),
+    )
 
 
 def exchange(blocks, axis):

time: 99.7 us -> 96.7 us (0.970)
  other arithmetic: 2.63 us -> 1.49 us
  local copies, waits for them, and re-layouts: 3.21 us -> 2.21 us
    reduce_sum x3, other arithmetic: 2.45 us -> 1.31 us  [added(): return jnp.sum(parts.astype(jnp.float32), axis=0)]
where the time goes in v2:
time: 96.7 us; the launch traced here: 96.3 us
  blocking collectives  40.5 us (42%)
  starting transfers between devices  19.2 us (20%)
  waiting for transfers between devices  16.4 us (17%)
  Pallas kernels  15 us (16%)
  local copies, waits for them, and re-layouts  2.21 us (2%)
  other arithmetic  1.49 us (2%)
  between operations  1.48 us (2%)
    all_to_all x2, blocking collectives, exchange(): return lax.all_to_all(blocks, axis, 0, 0, tiled=True)  40.5 us
    ppermute x2, starting transfers between devices, other_core(): return lax.ppermute(value, 'c', [(0, 1), (1, 0)])  15.4 us
    all_to_all x1, waiting for transfers between devices, exchange(): return lax.all_to_all(blocks, axis, 0, 0, tiled=True)  13.5 us
    pallas_call x1, Pallas kernels, backward(): pl.pallas_call(backward_kernel, out_shape=(jax.ShapeDtypeStruct((CAP, WIN...  8.85 us
    pallas_call x1, Pallas kernels, forward(): pl.pallas_call(forward_kernel, out_shape=(pltpu.VMEM((CAP, WIN, H * WIN),...  6.12 us
    all_to_all x1, starting transfers between devices, exchange(): return lax.all_to_all(blocks, axis, 0, 0, tiled=True)  3.75 us
    ppermute x2, waiting for transfers between devices, other_core(): return lax.ppermute(value, 'c', [(0, 1), (1, 0)])  2.92 us
  transfers between devices with their start and end apart: 3, of which 3 were waited for; matrix products, arithmetic and copies ran while one was open for 2% of the time, Pallas kernels for 0%

profile of v2, /device:TPU:1, one launch (start us, length us, event | category | flops | bytes accessed | tf_op | source)
XLA Modules:
  0.0 96.3 jit_solution(13478816315037826653)
XLA Ops:
  1.3 6.1 %shard_map.118 = (f32[5,64,512]{2,1,0:T(8,128)S(1)}, bf16[320,640]{1,0:T(8,128)(2,1)S(1)}, bf16[208,16,128]{2,1,0:T(8,128)(2,1)S(1)}, bf16[208,16,128]{2,1,0:T(8,128)(2,1)S(1)}) custom-call(s32[1]{0:T(128)S(6)} %copy.16.count_ref, s32[1]{0:T(128)} %bitcast.core_ref, bf16[5,64,640]{2,1,0:T(8,128)(2,1)} %q_hbm.3, bf16[5,64,640]{2,1,0:T(8,128)(2,1)} %k_hbm.3, ...), custom_call_target="tpu_custom_call" | custom-call | flops 800000000 | bytes 5000000 | tf_op jit(solution)/shard_map/pallas_call | solution.py:226
  7.4 8.8 %collective-permute-start = (bf16[208,16,128]{2,1,0:T(8,128)(2,1)S(1)}, bf16[208,16,128]{2,1,0:T(8,128)(2,1)S(1)}, u32[]{:S(2)}, u32[]{:S(2)}) collective-permute-start(bf16[208,16,128]{2,1,0:T(8,128)(2,1)S(1)} %get-tuple-element.17), channel_id=1, source_target_pairs={{0,16},{16,0},{1,17},{17,1},{2,18},{18,2},{3,19},{19,3},{4,20},{20... | collective-permute-start | bytes 2555912 | tf_op jit(solution)/shard_map/ppermute | solution.py:290
  16.2 2.0 %collective-permute-done = bf16[208,16,128]{2,1,0:T(8,128)(2,1)S(1)} collective-permute-done((bf16[208,16,128]{2,1,0:T(8,128)(2,1)S(1)}, bf16[208,16,128]{2,1,0:T(8,128)(2,1)S(1)}, u32[]{:S(2)}, u32[]{:S(2)}) %collective-permute-start) | collective-permute-done | bytes 852000 | tf_op jit(solution)/shard_map/ppermute | solution.py:290
  18.2 1.2 %reduce_sum.33 = bf16[208,16,128]{2,1,0:T(8,128)(2,1)} add(bf16[208,16,128]{2,1,0:T(8,128)(2,1)S(1)} %get-tuple-element.16, bf16[208,16,128]{2,1,0:T(8,128)(2,1)S(1)} %collective-permute-done) | non-fusion elementwise | flops 425984 | bytes 2555904 | tf_op jit(solution)/shard_map/reduce_sum | solution.py:294
  19.4 0.0 copy-start
  19.4 3.8 %all-to-all-start = ((bf16[16,13,16,128]{3,2,1,0:T(8,128)(2,1)}), bf16[16,13,16,128]{3,2,1,0:T(8,128)(2,1)S(1)}, u32[]{:S(2)}, u32[]{:S(2)}) async-start(bf16[16,13,16,128]{3,2,1,0:T(8,128)(2,1)} %bitcast.2), calls=%async_computation | async-start | bytes 1703936 | tf_op jit(solution)/shard_map/all_to_all | solution.py:286
  23.1 0.0 copy-done
  23.1 0.1 reshape.64
  23.2 0.0 copy-start.1
  23.3 0.1 pad.18.clone
  23.3 0.6 copy-done.1
  23.9 0.1 maximum_maximum_fusion
  24.1 13.5 %all-to-all-done = bf16[16,13,16,128]{3,2,1,0:T(8,128)(2,1)S(1)} async-done(((bf16[16,13,16,128]{3,2,1,0:T(8,128)(2,1)}), bf16[16,13,16,128]{3,2,1,0:T(8,128)(2,1)S(1)}, u32[]{:S(2)}, u32[]{:S(2)}) %all-to-all-start) | async-done | bytes 852000 | tf_op jit(solution)/shard_map/all_to_all | solution.py:286
  37.6 0.1 reduce_sum.34
  37.8 24.2 %all_to_all.15 = bf16[16,26,128]{2,1,0:T(8,128)(2,1)S(1)} all-to-all(bf16[16,26,128]{2,1,0:T(8,128)(2,1)S(1)} %copy.14), channel_id=1, replica_groups=mesh['z'=16,'c'=2,'y'=4,'x'=4] {'z'}, dimensions={0} | all-to-all | bytes 212992 | tf_op jit(solution)/shard_map/all_to_all | solution.py:286
  62.2 0.1 broadcast_in_dim.24
  62.3 16.3 %all_to_all.16.near_ref = bf16[16,15,16,128]{3,2,1,0:T(8,128)(2,1)S(1)} all-to-all(bf16[16,15,16,128]{3,2,1,0:T(8,128)(2,1)S(1)} %broadcast_in_dim.24), channel_id=1, replica_groups=mesh['z'=16,'c'=2,'y'=4,'x'=4] {'y','x'}, dimensions={0} | all-to-all | bytes 1966080 | tf_op jit(solution)/shard_map/all_to_all | solution.py:286
  78.6 6.7 %collective-permute-start.1 = (bf16[16,15,16,128]{3,2,1,0:T(8,128)(2,1)S(1)}, bf16[16,15,16,128]{3,2,1,0:T(8,128)(2,1)S(1)}, u32[]{:S(2)}, u32[]{:S(2)}) collective-permute-start(bf16[16,15,16,128]{3,2,1,0:T(8,128)(2,1)S(1)} %all_to_all.16.near_ref), channel_id=1, source_target_pairs={{0,16},{16,0},{1,17},{17,1},{2,18},{18,2},{3,19},{19,3},{4,20},{20... | collective-permute-start | bytes 2949128 | tf_op jit(solution)/shard_map/ppermute | solution.py:290
  85.3 0.7 reshape.66
  86.0 0.5 slice_bitcast_fusion.1
  86.5 0.9 collective-permute-done.1.far_ref
  87.5 8.8 %shard_map.119 = (bf16[5,64,1280]{2,1,0:T(8,128)(2,1)}, bf16[5,64,640]{2,1,0:T(8,128)(2,1)}, bf16[5,64,640]{2,1,0:T(8,128)(2,1)}, bf16[5,64,640]{2,1,0:T(8,128)(2,1)}) custom-call(s32[1]{0:T(128)S(6)} %copy.16.count_ref, s32[1]{0:T(128)} %bitcast.core_ref, bf16[5,64,640]{2,1,0:T(8,128)(2,1)} %q_hbm.3, bf16[5,64,640]{2,1,0:T(8,128)(2,1)} %k_hbm.3, ...), custom_call_target="tpu_custom_call" | custom-call | flops 1500000000 | bytes 8000000 | tf_op jit(solution)/shard_map/pallas_call | solution.py:254
  (17 shorter events, 0.3 us)
Async XLA Ops:
  7.4 10.8 %collective-permute-start = (bf16[208,16,128]{2,1,0:T(8,128)(2,1)S(1)}, bf16[208,16,128]{2,1,0:T(8,128)(2,1)S(1)}, u32[]{:S(2)}, u32[]{:S(2)}) collective-permute-start(bf16[208,16,128]{2,1,0:T(8,128)(2,1)S(1)} %get-tuple-element.17), channel_id=1, source_target_pairs={{0,16},{16,0},{1,17},{17,1},{2,18},{18,2},{3,19},{19,3},{4,20},{20... | collective-permute-start | bytes 2555912 | tf_op jit(solution)/shard_map/ppermute | solution.py:290
  19.4 3.8 %copy-start = (bf16[20,1280]{1,0:T(8,128)(2,1)S(1)}, bf16[20,1280]{1,0:T(8,128)(2,1)}, u32[]{:S(2)}) copy-start(bf16[20,1280]{1,0:T(8,128)(2,1)} %param.11) | copy-start | bytes 153604
  19.4 18.2 %all-to-all-start = ((bf16[16,13,16,128]{3,2,1,0:T(8,128)(2,1)}), bf16[16,13,16,128]{3,2,1,0:T(8,128)(2,1)S(1)}, u32[]{:S(2)}, u32[]{:S(2)}) async-start(bf16[16,13,16,128]{3,2,1,0:T(8,128)(2,1)} %bitcast.2), calls=%async_computation | async-start | bytes 1703936 | tf_op jit(solution)/shard_map/all_to_all | solution.py:286
  23.2 0.7 copy-start.1
  78.6 8.8 %collective-permute-start.1 = (bf16[16,15,16,128]{3,2,1,0:T(8,128)(2,1)S(1)}, bf16[16,15,16,128]{3,2,1,0:T(8,128)(2,1)S(1)}, u32[]{:S(2)}, u32[]{:S(2)}) collective-permute-start(bf16[16,15,16,128]{3,2,1,0:T(8,128)(2,1)S(1)} %all_to_all.16.near_ref), channel_id=1, source_target_pairs={{0,16},{16,0},{1,17},{17,1},{2,18},{18,2},{3,19},{19,3},{4,20},{20... | collective-permute-start | bytes 2949128 | tf_op jit(solution)/shard_map/ppermute | solution.py:290

commit v3 on v2

--- a/solution.py
+++ b/solution.py
@@ -57,7 +57,8 @@
 def bias_pick():
     from_place = lax.broadcasted_iota(jnp.int32, (D, 128), 0)
     to_lane = lax.broadcasted_iota(jnp.int32, (D, 128), 1)
-    return jnp.where(lax.rem(from_place, BIAS) == to_lane, 1.0, 0.0).astype(jnp.bfloat16)
+    owner = (from_place * 1639) >> 16
+    return jnp.where(from_place - owner * BIAS == to_lane, 1.0, 0.0).astype(jnp.bfloat16)
 
 
 def bias_owner(core):
@@ -68,25 +69,21 @@
 
 def forward_kernel(
     count_ref, core_ref, q_hbm, k_hbm, v_hbm, g_hbm, probs_ref, att_ref, own_ref, other_ref,
-    q_ref, k_ref, v_ref, g_ref, acc, in_sems, g_sem,
+    q_ref, k_ref, v_ref, g_ref, acc, in_sems,
 ):
     count, my_core = count_ref[0], core_ref[0]
     masks = [head_masks(pair) for pair in range(PAIRS)]
     moves = [
-        [
-            pltpu.make_async_copy(far.at[w], near.at[w], in_sems.at[which, w])
-            for which, (far, near) in enumerate(((q_hbm, q_ref), (k_hbm, k_ref), (v_hbm, v_ref)))
-        ]
-        for w in range(CAP)
+        pltpu.make_async_copy(there, here, in_sems.at[at])
+        for at, (there, here) in enumerate(
+            ((q_hbm, q_ref), (k_hbm, k_ref), (v_hbm, v_ref), (g_hbm, g_ref))
+        )
     ]
-    for window_moves in moves:
-        for move in window_moves:
-            move.start()
-    g_move = pltpu.make_async_copy(g_hbm, g_ref, g_sem)
-    g_move.start()
+    for move in moves:
+        move.start()
+    for move in moves[:3]:
+        move.wait()
     for w in range(CAP):
-        for move in moves[w]:
-            move.wait()
         rows = slice(WIN * w, WIN * (w + 1))
         tiles = [None] * (PAIRS + 1)
         for pair in range(PAIRS):
@@ -95,7 +92,7 @@
             q_both = stacked(q_ref[w, :, span], mask_a, mask_b)
             scores = mm(k_ref[w, :, span], q_both, NT) * SCALE
             raised = jnp.exp(scores - jnp.max(scores, axis=0, keepdims=True))
-            probs = raised / jnp.sum(raised, axis=0, keepdims=True)
+            probs = raised * (1.0 / jnp.sum(raised, axis=0, keepdims=True))
             probs_ref[w, :, 128 * pair : 128 * (pair + 1)] = probs
             both = mm(probs.astype(jnp.bfloat16), v_ref[w, :, span], TN)
             add_span(tiles, pair, both[:WIN] * mask_a + both[WIN:] * mask_b)
@@ -105,7 +102,7 @@
     row_of = lax.broadcasted_iota(jnp.int32, (16, CAP * WIN), 1)
     live_rows = jnp.where(row_of < count * WIN, 1.0, 0.0).astype(jnp.bfloat16)
     left = jnp.concatenate([att_ref[...].T, live_rows], axis=0)
-    g_move.wait()
+    moves[3].wait()
     bias_parts = []
     for block in range(0, BLOCKS, 2):
         made = mm(left, g_ref[:, 128 * block : 128 * (block + 2)], NN)
@@ -170,7 +167,6 @@
     for move in moves:
         move.wait()
     grad_att[...] = mm(g_ref[...], weight_ref[...], NT).astype(jnp.bfloat16)
-    results = ((dq_ref, dq_hbm), (dk_ref, dk_hbm), (dv_ref, dv_hbm))
     for w in range(CAP):
         rows = slice(WIN * w, WIN * (w + 1))
         keep = jnp.where(w < count, 1.0, 0.0)
@@ -194,10 +190,10 @@
             dq_ref[w, :, cols] = (dq_tiles[at] * (keep * SCALE)).astype(jnp.bfloat16)
             dk_ref[w, :, cols] = (dk_tiles[at] * (keep * SCALE)).astype(jnp.bfloat16)
             dv_ref[w, :, cols] = (dv_tiles[at] * keep).astype(jnp.bfloat16)
-        for which, (made, out) in enumerate(results):
-            move = pltpu.make_async_copy(made.at[w], out.at[w], out_sems.at[which, w])
-            move.start()
-            back.append(move)
+    results = ((dq_ref, dq_hbm), (dk_ref, dk_hbm), (dv_ref, dv_hbm))
+    for which, (made, out) in enumerate(results):
+        back.append(pltpu.make_async_copy(made, out, out_sems.at[which]))
+        back[-1].start()
     for move in back:
         move.wait()
 
@@ -239,8 +235,7 @@
             pltpu.VMEM((CAP, WIN, ATTN), jnp.bfloat16),
             pltpu.VMEM((CAP * WIN, D), jnp.bfloat16),
             pltpu.VMEM((BLOCKS, ATTN, 128), jnp.float32),
-            pltpu.SemaphoreType.DMA((3, CAP)),
-            pltpu.SemaphoreType.DMA,
+            pltpu.SemaphoreType.DMA((4,)),
         ],
         compiler_params=pltpu.CompilerParams(vmem_limit_bytes=VMEM_LIMIT),
         cost_estimate=pl.CostEstimate(
@@ -269,7 +264,7 @@
             pltpu.VMEM((BLOCKS, ATTN, 128), jnp.float32),
             pltpu.VMEM((ATTN, D), jnp.bfloat16),
             pltpu.SemaphoreType.DMA((4,)),
-            pltpu.SemaphoreType.DMA((3, CAP)),
+            pltpu.SemaphoreType.DMA((3,)),
             pltpu.SemaphoreType.DMA,
         ],
         compiler_params=pltpu.CompilerParams(vmem_limit_bytes=VMEM_LIMIT),

time: 96.7 us -> 95.6 us (0.989)
  Pallas kernels: 15 us -> 13.9 us
    pallas_call x1, Pallas kernels: 6.12 us -> 4.84 us  [forward(): pl.pallas_call(forward_kernel, out_shape=(pltpu.VMEM((CAP, WIN, H * WIN),...]
where the time goes in v3:
time: 95.6 us; the launch traced here: 95.2 us
  blocking collectives  40.5 us (42%)
  starting transfers between devices  19.2 us (20%)
  waiting for transfers between devices  16.4 us (17%)
  Pallas kernels  13.9 us (15%)
  local copies, waits for them, and re-layouts  2.21 us (2%)
  other arithmetic  1.49 us (2%)
  between operations  1.48 us (2%)
    all_to_all x2, blocking collectives, exchange(): return lax.all_to_all(blocks, axis, 0, 0, tiled=True)  40.5 us
    ppermute x2, starting transfers between devices, other_core(): return lax.ppermute(value, 'c', [(0, 1), (1, 0)])  15.5 us
    all_to_all x1, waiting for transfers between devices, exchange(): return lax.all_to_all(blocks, axis, 0, 0, tiled=True)  13.5 us
    pallas_call x1, Pallas kernels, backward(): pl.pallas_call(backward_kernel, out_shape=(jax.ShapeDtypeStruct((CAP, WIN...  9.02 us
    pallas_call x1, Pallas kernels, forward(): pl.pallas_call(forward_kernel, out_shape=(pltpu.VMEM((CAP, WIN, H * WIN),...  4.84 us
    all_to_all x1, starting transfers between devices, exchange(): return lax.all_to_all(blocks, axis, 0, 0, tiled=True)  3.75 us
    ppermute x2, waiting for transfers between devices, other_core(): return lax.ppermute(value, 'c', [(0, 1), (1, 0)])  2.92 us
  transfers between devices with their start and end apart: 3, of which 3 were waited for; matrix products, arithmetic and copies ran while one was open for 2% of the time, Pallas kernels for 0%

profile of v3, /device:TPU:1, one launch (start us, length us, event | category | flops | bytes accessed | tf_op | source)
XLA Modules:
  0.0 95.2 jit_solution(9176832544346000085)
XLA Ops:
  1.3 4.8 %shard_map.118 = (f32[5,64,512]{2,1,0:T(8,128)S(1)}, bf16[320,640]{1,0:T(8,128)(2,1)S(1)}, bf16[208,16,128]{2,1,0:T(8,128)(2,1)S(1)}, bf16[208,16,128]{2,1,0:T(8,128)(2,1)S(1)}) custom-call(s32[1]{0:T(128)S(6)} %copy.16.count_ref, s32[1]{0:T(128)} %bitcast.core_ref, bf16[5,64,640]{2,1,0:T(8,128)(2,1)} %q_hbm.3, bf16[5,64,640]{2,1,0:T(8,128)(2,1)} %k_hbm.3, ...), custom_call_target="tpu_custom_call" | custom-call | flops 800000000 | bytes 5000000 | tf_op jit(solution)/shard_map/pallas_call | solution.py:222
  6.1 8.8 %collective-permute-start = (bf16[208,16,128]{2,1,0:T(8,128)(2,1)S(1)}, bf16[208,16,128]{2,1,0:T(8,128)(2,1)S(1)}, u32[]{:S(2)}, u32[]{:S(2)}) collective-permute-start(bf16[208,16,128]{2,1,0:T(8,128)(2,1)S(1)} %get-tuple-element.17), channel_id=1, source_target_pairs={{0,16},{16,0},{1,17},{17,1},{2,18},{18,2},{3,19},{19,3},{4,20},{20... | collective-permute-start | bytes 2555912 | tf_op jit(solution)/shard_map/ppermute | solution.py:285
  14.9 2.0 %collective-permute-done = bf16[208,16,128]{2,1,0:T(8,128)(2,1)S(1)} collective-permute-done((bf16[208,16,128]{2,1,0:T(8,128)(2,1)S(1)}, bf16[208,16,128]{2,1,0:T(8,128)(2,1)S(1)}, u32[]{:S(2)}, u32[]{:S(2)}) %collective-permute-start) | collective-permute-done | bytes 852000 | tf_op jit(solution)/shard_map/ppermute | solution.py:285
  16.9 1.2 %reduce_sum.33 = bf16[208,16,128]{2,1,0:T(8,128)(2,1)} add(bf16[208,16,128]{2,1,0:T(8,128)(2,1)S(1)} %get-tuple-element.16, bf16[208,16,128]{2,1,0:T(8,128)(2,1)S(1)} %collective-permute-done) | non-fusion elementwise | flops 425984 | bytes 2555904 | tf_op jit(solution)/shard_map/reduce_sum | solution.py:289
  18.1 0.0 copy-start
  18.1 3.8 %all-to-all-start = ((bf16[16,13,16,128]{3,2,1,0:T(8,128)(2,1)}), bf16[16,13,16,128]{3,2,1,0:T(8,128)(2,1)S(1)}, u32[]{:S(2)}, u32[]{:S(2)}) async-start(bf16[16,13,16,128]{3,2,1,0:T(8,128)(2,1)} %bitcast.2), calls=%async_computation | async-start | bytes 1703936 | tf_op jit(solution)/shard_map/all_to_all | solution.py:281
  21.9 0.0 copy-done
  21.9 0.1 reshape.64
  22.0 0.0 copy-start.1
  22.0 0.1 pad.18.clone
  22.1 0.6 copy-done.1
  22.6 0.1 maximum_maximum_fusion
  22.8 13.5 %all-to-all-done = bf16[16,13,16,128]{3,2,1,0:T(8,128)(2,1)S(1)} async-done(((bf16[16,13,16,128]{3,2,1,0:T(8,128)(2,1)}), bf16[16,13,16,128]{3,2,1,0:T(8,128)(2,1)S(1)}, u32[]{:S(2)}, u32[]{:S(2)}) %all-to-all-start) | async-done | bytes 852000 | tf_op jit(solution)/shard_map/all_to_all | solution.py:281
  36.3 0.1 reduce_sum.34
  36.5 24.2 %all_to_all.15 = bf16[16,26,128]{2,1,0:T(8,128)(2,1)S(1)} all-to-all(bf16[16,26,128]{2,1,0:T(8,128)(2,1)S(1)} %copy.14), channel_id=1, replica_groups=mesh['z'=16,'c'=2,'y'=4,'x'=4] {'z'}, dimensions={0} | all-to-all | bytes 212992 | tf_op jit(solution)/shard_map/all_to_all | solution.py:281
  60.9 0.1 broadcast_in_dim.24
  61.0 16.3 %all_to_all.16.near_ref = bf16[16,15,16,128]{3,2,1,0:T(8,128)(2,1)S(1)} all-to-all(bf16[16,15,16,128]{3,2,1,0:T(8,128)(2,1)S(1)} %broadcast_in_dim.24), channel_id=1, replica_groups=mesh['z'=16,'c'=2,'y'=4,'x'=4] {'y','x'}, dimensions={0} | all-to-all | bytes 1966080 | tf_op jit(solution)/shard_map/all_to_all | solution.py:281
  77.3 6.7 %collective-permute-start.1 = (bf16[16,15,16,128]{3,2,1,0:T(8,128)(2,1)S(1)}, bf16[16,15,16,128]{3,2,1,0:T(8,128)(2,1)S(1)}, u32[]{:S(2)}, u32[]{:S(2)}) collective-permute-start(bf16[16,15,16,128]{3,2,1,0:T(8,128)(2,1)S(1)} %all_to_all.16.near_ref), channel_id=1, source_target_pairs={{0,16},{16,0},{1,17},{17,1},{2,18},{18,2},{3,19},{19,3},{4,20},{20... | collective-permute-start | bytes 2949128 | tf_op jit(solution)/shard_map/ppermute | solution.py:285
  84.1 0.7 reshape.66
  84.7 0.5 slice_bitcast_fusion.1
  85.3 0.9 collective-permute-done.1.far_ref
  86.2 9.0 %shard_map.119 = (bf16[5,64,1280]{2,1,0:T(8,128)(2,1)}, bf16[5,64,640]{2,1,0:T(8,128)(2,1)}, bf16[5,64,640]{2,1,0:T(8,128)(2,1)}, bf16[5,64,640]{2,1,0:T(8,128)(2,1)}) custom-call(s32[1]{0:T(128)S(6)} %copy.16.count_ref, s32[1]{0:T(128)} %bitcast.core_ref, bf16[5,64,640]{2,1,0:T(8,128)(2,1)} %q_hbm.3, bf16[5,64,640]{2,1,0:T(8,128)(2,1)} %k_hbm.3, ...), custom_call_target="tpu_custom_call" | custom-call | flops 1500000000 | bytes 8000000 | tf_op jit(solution)/shard_map/pallas_call | solution.py:249
  (17 shorter events, 0.3 us)
Async XLA Ops:
  6.1 10.8 %collective-permute-start = (bf16[208,16,128]{2,1,0:T(8,128)(2,1)S(1)}, bf16[208,16,128]{2,1,0:T(8,128)(2,1)S(1)}, u32[]{:S(2)}, u32[]{:S(2)}) collective-permute-start(bf16[208,16,128]{2,1,0:T(8,128)(2,1)S(1)} %get-tuple-element.17), channel_id=1, source_target_pairs={{0,16},{16,0},{1,17},{17,1},{2,18},{18,2},{3,19},{19,3},{4,20},{20... | collective-permute-start | bytes 2555912 | tf_op jit(solution)/shard_map/ppermute | solution.py:285
  18.1 3.8 %copy-start = (bf16[20,1280]{1,0:T(8,128)(2,1)S(1)}, bf16[20,1280]{1,0:T(8,128)(2,1)}, u32[]{:S(2)}) copy-start(bf16[20,1280]{1,0:T(8,128)(2,1)} %param.11) | copy-start | bytes 153604
  18.1 18.2 %all-to-all-start = ((bf16[16,13,16,128]{3,2,1,0:T(8,128)(2,1)}), bf16[16,13,16,128]{3,2,1,0:T(8,128)(2,1)S(1)}, u32[]{:S(2)}, u32[]{:S(2)}) async-start(bf16[16,13,16,128]{3,2,1,0:T(8,128)(2,1)} %bitcast.2), calls=%async_computation | async-start | bytes 1703936 | tf_op jit(solution)/shard_map/all_to_all | solution.py:281
  22.0 0.7 copy-start.1
  77.3 8.8 %collective-permute-start.1 = (bf16[16,15,16,128]{3,2,1,0:T(8,128)(2,1)S(1)}, bf16[16,15,16,128]{3,2,1,0:T(8,128)(2,1)S(1)}, u32[]{:S(2)}, u32[]{:S(2)}) collective-permute-start(bf16[16,15,16,128]{3,2,1,0:T(8,128)(2,1)S(1)} %all_to_all.16.near_ref), channel_id=1, source_target_pairs={{0,16},{16,0},{1,17},{17,1},{2,18},{18,2},{3,19},{19,3},{4,20},{20... | collective-permute-start | bytes 2949128 | tf_op jit(solution)/shard_map/ppermute | solution.py:285

commit v4 on v3

--- a/solution.py
+++ b/solution.py
@@ -67,12 +67,21 @@
     return (place >= seq * BIAS) & (place < (seq + 1) * BIAS)
 
 
+def row_order(my_core):
+    place = lax.broadcasted_iota(jnp.int32, (1, ATTN), 1)
+    half = jnp.where(place >= ATTN // 2, 1, 0)
+    core = jnp.where(half == 0, my_core, 1 - my_core)
+    inner = place - half * (ATTN // 2)
+    feature = (inner & (Z - 1)) * (CORES * ROWS) + core * ROWS + (inner >> 4)
+    rows = lax.broadcasted_iota(jnp.int32, (ATTN, ATTN), 0)
+    return jnp.where(rows == feature, 1.0, 0.0).astype(jnp.bfloat16)
+
+
 def forward_kernel(
     count_ref, core_ref, q_hbm, k_hbm, v_hbm, g_hbm, probs_ref, att_ref, own_ref, other_ref,
-    q_ref, k_ref, v_ref, g_ref, acc, in_sems,
+    q_ref, k_ref, v_ref, g_ref, natural, in_sems,
 ):
     count, my_core = count_ref[0], core_ref[0]
-    masks = [head_masks(pair) for pair in range(PAIRS)]
     moves = [
         pltpu.make_async_copy(there, here, in_sems.at[at])
         for at, (there, here) in enumerate(
@@ -81,6 +90,8 @@
     ]
     for move in moves:
         move.start()
+    order = row_order(my_core)
+    masks = [head_masks(pair) for pair in range(PAIRS)]
     for move in moves[:3]:
         move.wait()
     for w in range(CAP):
@@ -98,25 +109,27 @@
             add_span(tiles, pair, both[:WIN] * mask_a + both[WIN:] * mask_b)
         keep = jnp.where(w < count, 1.0, 0.0)
         for at, tile in enumerate(tiles):
-            att_ref[rows, 128 * at : 128 * (at + 1)] = (tile * keep).astype(jnp.bfloat16)
+            natural[rows, 128 * at : 128 * (at + 1)] = (tile * keep).astype(jnp.bfloat16)
+    attended = mm(natural[...], order, NN).astype(jnp.bfloat16)
+    att_ref[...] = attended
     row_of = lax.broadcasted_iota(jnp.int32, (16, CAP * WIN), 1)
     live_rows = jnp.where(row_of < count * WIN, 1.0, 0.0).astype(jnp.bfloat16)
-    left = jnp.concatenate([att_ref[...].T, live_rows], axis=0)
+    left = jnp.concatenate([attended.T, live_rows], axis=0)
     moves[3].wait()
     bias_parts = []
-    for block in range(0, BLOCKS, 2):
-        made = mm(left, g_ref[:, 128 * block : 128 * (block + 2)], NN)
-        acc[block] = made[:ATTN, :128]
-        acc[block + 1] = made[:ATTN, 128:]
+    for start in range(0, BLOCKS, 2):
+        made = mm(left, g_ref[:, 128 * start : 128 * (start + 2)], NN)
+        for block in range(2):
+            cols = slice(128 * block, 128 * (block + 1))
+            for row in range(ROWS):
+                unit = row * BLOCKS + start + block
+                own_ref[unit] = made[Z * row : Z * (row + 1), cols].astype(jnp.bfloat16)
+                second = ATTN // 2 + Z * row
+                other_ref[unit] = made[second : second + Z, cols].astype(jnp.bfloat16)
         bias_parts.append(made[ATTN : ATTN + 1])
     bias_row = jnp.concatenate(bias_parts, axis=1)
     pick = bias_pick()
     for core, wire_ref in ((my_core, own_ref), (1 - my_core, other_ref)):
-        for row in range(ROWS):
-            for block in range(BLOCKS):
-                wire_ref[row * BLOCKS + block] = acc[
-                    block, pl.ds(core * ROWS + row, Z, stride=CORES * ROWS), :
-                ].astype(jnp.bfloat16)
         owned = jnp.where(bias_owner(core), jnp.broadcast_to(bias_row, (Z, D)), 0.0)
         wire_ref[ROWS * BLOCKS] = mm(owned.astype(jnp.bfloat16), pick, NN).astype(jnp.bfloat16)
         for unit in range(ROWS * BLOCKS + 1, UNITS):
@@ -127,7 +140,7 @@
     count_ref, core_ref, q_hbm, k_hbm, v_hbm, g_hbm, probs_ref, att_ref, near_ref, far_ref,
     enc_hbm, dq_hbm, dk_hbm, dv_hbm,
     q_ref, k_ref, v_ref, g_ref, enc_ref, dq_ref, dk_ref, dv_ref,
-    grad_att, wide, weight_ref, in_sems, out_sems, enc_sem,
+    grad_att, weight_ref, in_sems, out_sems,
 ):
     count, my_core = count_ref[0], core_ref[0]
     moves = [
@@ -138,35 +151,26 @@
     ]
     for move in moves:
         move.start()
+    order = row_order(my_core)
     masks = [head_masks(pair) for pair in range(PAIRS)]
     bias_pieces = []
-    for held, core in ((near_ref, my_core), (far_ref, 1 - my_core)):
+    for which, (held, core) in enumerate(((near_ref, my_core), (far_ref, 1 - my_core))):
         for unit in range(ROWS * BLOCKS + 1):
             owner, at = divmod(unit, PART)
             piece = held[owner, at]
             row, block = divmod(unit, BLOCKS)
             if row < ROWS:
-                wide[block, pl.ds(core * ROWS + row, Z, stride=CORES * ROWS), :] = piece.astype(
-                    jnp.float32
-                )
+                first = which * (ATTN // 2) + Z * row
+                weight_ref[first : first + Z, 128 * block : 128 * (block + 1)] = piece
             else:
                 spread = mm(piece, bias_pick(), NT)
                 bias_pieces.append(jnp.where(bias_owner(core), spread, 0.0))
     bias = jnp.sum(bias_pieces[0] + bias_pieces[1], axis=0, keepdims=True)
-    for block in range(BLOCKS):
-        weight_ref[:, 128 * block : 128 * (block + 1)] = wide[block].astype(jnp.bfloat16)
-    live_rows = lax.broadcasted_iota(jnp.int32, (CAP * WIN, 1), 0) < count * WIN
-    for block in range(0, BLOCKS, 2):
-        cols = slice(128 * block, 128 * (block + 2))
-        encoded = mm(att_ref[...], weight_ref[:, cols], NN) + bias[:, cols]
-        encoded = jnp.where(live_rows, encoded, 0.0).astype(jnp.bfloat16)
-        for w in range(CAP):
-            enc_ref[w, :, cols] = encoded[WIN * w : WIN * (w + 1)]
-    back = [pltpu.make_async_copy(enc_ref, enc_hbm, enc_sem)]
-    back[0].start()
     for move in moves:
         move.wait()
-    grad_att[...] = mm(g_ref[...], weight_ref[...], NT).astype(jnp.bfloat16)
+    ordered = mm(g_ref[...], weight_ref[...], NT).astype(jnp.bfloat16)
+    grad_att[...] = mm(ordered, order, NT).astype(jnp.bfloat16)
+    live_rows = lax.broadcasted_iota(jnp.int32, (CAP * WIN, 1), 0) < count * WIN
     for w in range(CAP):
         rows = slice(WIN * w, WIN * (w + 1))
         keep = jnp.where(w < count, 1.0, 0.0)
@@ -190,10 +194,19 @@
             dq_ref[w, :, cols] = (dq_tiles[at] * (keep * SCALE)).astype(jnp.bfloat16)
             dk_ref[w, :, cols] = (dk_tiles[at] * (keep * SCALE)).astype(jnp.bfloat16)
             dv_ref[w, :, cols] = (dv_tiles[at] * keep).astype(jnp.bfloat16)
-    results = ((dq_ref, dq_hbm), (dk_ref, dk_hbm), (dv_ref, dv_hbm))
-    for which, (made, out) in enumerate(results):
-        back.append(pltpu.make_async_copy(made, out, out_sems.at[which]))
-        back[-1].start()
+        cols = slice(256 * w, 256 * (w + 1))
+        encoded = mm(att_ref[...], weight_ref[:, cols], NN) + bias[:, cols]
+        encoded = jnp.where(live_rows, encoded, 0.0).astype(jnp.bfloat16)
+        for window in range(CAP):
+            enc_ref[window, :, cols] = encoded[WIN * window : WIN * (window + 1)]
+    back = [
+        pltpu.make_async_copy(made, out, out_sems.at[at])
+        for at, (made, out) in enumerate(
+            ((enc_ref, enc_hbm), (dq_ref, dq_hbm), (dk_ref, dk_hbm), (dv_ref, dv_hbm))
+        )
+    ]
+    for move in back:
+        move.start()
     for move in back:
         move.wait()
 
@@ -219,57 +232,58 @@
 
 
 def forward(count, core, queries, key_rows, value_rows, grads):
+    rows = pltpu.VMEM((CAP, WIN, ATTN), jnp.bfloat16)
+    wire = pltpu.VMEM((UNITS, Z, 128), jnp.bfloat16)
     return pl.pallas_call(
         forward_kernel,
         out_shape=(
             pltpu.VMEM((CAP, WIN, H * WIN), jnp.float32),
             pltpu.VMEM((CAP * WIN, ATTN), jnp.bfloat16),
-            pltpu.VMEM((UNITS, Z, 128), jnp.bfloat16),
-            pltpu.VMEM((UNITS, Z, 128), jnp.bfloat16),
+            wire,
+            wire,
         ),
         in_specs=[smem_spec()] * 2 + [hbm_spec()] * 4,
         out_specs=(vmem_spec(),) * 4,
         scratch_shapes=[
-            pltpu.VMEM((CAP, WIN, ATTN), jnp.bfloat16),
-            pltpu.VMEM((CAP, WIN, ATTN), jnp.bfloat16),
-            pltpu.VMEM((CAP, WIN, ATTN), jnp.bfloat16),
+            rows,
+            rows,
+            rows,
             pltpu.VMEM((CAP * WIN, D), jnp.bfloat16),
-            pltpu.VMEM((BLOCKS, ATTN, 128), jnp.float32),
+            pltpu.VMEM((CAP * WIN, ATTN), jnp.bfloat16),
             pltpu.SemaphoreType.DMA((4,)),
         ],
         compiler_params=pltpu.CompilerParams(vmem_limit_bytes=VMEM_LIMIT),
         cost_estimate=pl.CostEstimate(
-            flops=800_000_000, bytes_accessed=5_000_000, transcendentals=200_000
+            flops=1_000_000_000, bytes_accessed=5_000_000, transcendentals=200_000
         ),
     )(count, core, *(in_hbm(array) for array in (queries, key_rows, value_rows, grads)))
 
 
 def backward(count, core, queries, key_rows, value_rows, grads, probs, attended, near, far):
     rows = jax.ShapeDtypeStruct((CAP, WIN, ATTN), jnp.bfloat16)
+    held = pltpu.VMEM((CAP, WIN, ATTN), jnp.bfloat16)
     return pl.pallas_call(
         backward_kernel,
         out_shape=(jax.ShapeDtypeStruct((CAP, WIN, D), jnp.bfloat16), rows, rows, rows),
         in_specs=[smem_spec()] * 2 + [hbm_spec()] * 4 + [vmem_spec()] * 4,
         out_specs=(hbm_spec(),) * 4,
         scratch_shapes=[
-            pltpu.VMEM((CAP, WIN, ATTN), jnp.bfloat16),
-            pltpu.VMEM((CAP, WIN, ATTN), jnp.bfloat16),
-            pltpu.VMEM((CAP, WIN, ATTN), jnp.bfloat16),
+            held,
+            held,
+            held,
             pltpu.VMEM((CAP * WIN, D), jnp.bfloat16),
             pltpu.VMEM((CAP, WIN, D), jnp.bfloat16),
-            pltpu.VMEM((CAP, WIN, ATTN), jnp.bfloat16),
-            pltpu.VMEM((CAP, WIN, ATTN), jnp.bfloat16),
-            pltpu.VMEM((CAP, WIN, ATTN), jnp.bfloat16),
+            held,
+            held,
+            held,
             pltpu.VMEM((CAP * WIN, ATTN), jnp.bfloat16),
-            pltpu.VMEM((BLOCKS, ATTN, 128), jnp.float32),
             pltpu.VMEM((ATTN, D), jnp.bfloat16),
             pltpu.SemaphoreType.DMA((4,)),
-            pltpu.SemaphoreType.DMA((3,)),
-            pltpu.SemaphoreType.DMA,
+            pltpu.SemaphoreType.DMA((4,)),
         ],
         compiler_params=pltpu.CompilerParams(vmem_limit_bytes=VMEM_LIMIT),
         cost_estimate=pl.CostEstimate(
-            flops=1_500_000_000, bytes_accessed=8_000_000, transcendentals=0
+            flops=1_700_000_000, bytes_accessed=8_000_000, transcendentals=0
         ),
     )(
         count, core, *(in_hbm(array) for array in (queries, key_rows, value_rows, grads)),

time: 95.6 us -> 95.1 us (level)
  no operation moved by 1% of the time
where the time goes in v4:
time: 95.1 us; the launch traced here: 94.7 us
  blocking collectives  40.5 us (43%)
  starting transfers between devices  19.2 us (20%)
  waiting for transfers between devices  16.4 us (17%)
  Pallas kernels  13.4 us (14%)
  local copies, waits for them, and re-layouts  2.21 us (2%)
  other arithmetic  1.49 us (2%)
  between operations  1.48 us (2%)
    all_to_all x2, blocking collectives, exchange(): return lax.all_to_all(blocks, axis, 0, 0, tiled=True)  40.5 us
    ppermute x2, starting transfers between devices, other_core(): return lax.ppermute(value, 'c', [(0, 1), (1, 0)])  15.5 us
    all_to_all x1, waiting for transfers between devices, exchange(): return lax.all_to_all(blocks, axis, 0, 0, tiled=True)  13.5 us
    pallas_call x1, Pallas kernels, backward(): pl.pallas_call(backward_kernel, out_shape=(jax.ShapeDtypeStruct((CAP, WIN...  8.38 us
    pallas_call x1, Pallas kernels, forward(): pl.pallas_call(forward_kernel, out_shape=(pltpu.VMEM((CAP, WIN, H * WIN),...  4.99 us
    all_to_all x1, starting transfers between devices, exchange(): return lax.all_to_all(blocks, axis, 0, 0, tiled=True)  3.75 us
    ppermute x2, waiting for transfers between devices, other_core(): return lax.ppermute(value, 'c', [(0, 1), (1, 0)])  2.92 us
  transfers between devices with their start and end apart: 3, of which 3 were waited for; matrix products, arithmetic and copies ran while one was open for 2% of the time, Pallas kernels for 0%

profile of v4, /device:TPU:1, one launch (start us, length us, event | category | flops | bytes accessed | tf_op | source)
XLA Modules:
  0.0 94.7 jit_solution(13954566317329212926)
XLA Ops:
  1.3 5.0 %shard_map.118 = (f32[5,64,512]{2,1,0:T(8,128)S(1)}, bf16[320,640]{1,0:T(8,128)(2,1)S(1)}, bf16[208,16,128]{2,1,0:T(8,128)(2,1)S(1)}, bf16[208,16,128]{2,1,0:T(8,128)(2,1)S(1)}) custom-call(s32[1]{0:T(128)S(6)} %copy.16.count_ref, s32[1]{0:T(128)} %bitcast.core_ref, bf16[5,64,640]{2,1,0:T(8,128)(2,1)} %q_hbm.3, bf16[5,64,640]{2,1,0:T(8,128)(2,1)} %k_hbm.3, ...), custom_call_target="tpu_custom_call" | custom-call | flops 1000000000 | bytes 5000000 | tf_op jit(solution)/shard_map/pallas_call | solution.py:237
  6.3 8.8 %collective-permute-start = (bf16[208,16,128]{2,1,0:T(8,128)(2,1)S(1)}, bf16[208,16,128]{2,1,0:T(8,128)(2,1)S(1)}, u32[]{:S(2)}, u32[]{:S(2)}) collective-permute-start(bf16[208,16,128]{2,1,0:T(8,128)(2,1)S(1)} %get-tuple-element.17), channel_id=1, source_target_pairs={{0,16},{16,0},{1,17},{17,1},{2,18},{18,2},{3,19},{19,3},{4,20},{20... | collective-permute-start | bytes 2555912 | tf_op jit(solution)/shard_map/ppermute | solution.py:299
  15.1 2.0 %collective-permute-done = bf16[208,16,128]{2,1,0:T(8,128)(2,1)S(1)} collective-permute-done((bf16[208,16,128]{2,1,0:T(8,128)(2,1)S(1)}, bf16[208,16,128]{2,1,0:T(8,128)(2,1)S(1)}, u32[]{:S(2)}, u32[]{:S(2)}) %collective-permute-start) | collective-permute-done | bytes 852000 | tf_op jit(solution)/shard_map/ppermute | solution.py:299
  17.1 1.2 %reduce_sum.33 = bf16[208,16,128]{2,1,0:T(8,128)(2,1)} add(bf16[208,16,128]{2,1,0:T(8,128)(2,1)S(1)} %get-tuple-element.16, bf16[208,16,128]{2,1,0:T(8,128)(2,1)S(1)} %collective-permute-done) | non-fusion elementwise | flops 425984 | bytes 2555904 | tf_op jit(solution)/shard_map/reduce_sum | solution.py:303
  18.2 0.0 copy-start
  18.2 3.8 %all-to-all-start = ((bf16[16,13,16,128]{3,2,1,0:T(8,128)(2,1)}), bf16[16,13,16,128]{3,2,1,0:T(8,128)(2,1)S(1)}, u32[]{:S(2)}, u32[]{:S(2)}) async-start(bf16[16,13,16,128]{3,2,1,0:T(8,128)(2,1)} %bitcast.2), calls=%async_computation | async-start | bytes 1703936 | tf_op jit(solution)/shard_map/all_to_all | solution.py:295
  22.0 0.0 copy-done
  22.0 0.1 reshape.64
  22.1 0.0 copy-start.1
  22.1 0.1 pad.18.clone
  22.2 0.6 copy-done.1
  22.8 0.1 maximum_maximum_fusion
  22.9 13.5 %all-to-all-done = bf16[16,13,16,128]{3,2,1,0:T(8,128)(2,1)S(1)} async-done(((bf16[16,13,16,128]{3,2,1,0:T(8,128)(2,1)}), bf16[16,13,16,128]{3,2,1,0:T(8,128)(2,1)S(1)}, u32[]{:S(2)}, u32[]{:S(2)}) %all-to-all-start) | async-done | bytes 852000 | tf_op jit(solution)/shard_map/all_to_all | solution.py:295
  36.5 0.1 reduce_sum.34
  36.7 24.2 %all_to_all.15 = bf16[16,26,128]{2,1,0:T(8,128)(2,1)S(1)} all-to-all(bf16[16,26,128]{2,1,0:T(8,128)(2,1)S(1)} %copy.14), channel_id=1, replica_groups=mesh['z'=16,'c'=2,'y'=4,'x'=4] {'z'}, dimensions={0} | all-to-all | bytes 212992 | tf_op jit(solution)/shard_map/all_to_all | solution.py:295
  61.1 0.1 broadcast_in_dim.24
  61.2 16.3 %all_to_all.16.near_ref = bf16[16,15,16,128]{3,2,1,0:T(8,128)(2,1)S(1)} all-to-all(bf16[16,15,16,128]{3,2,1,0:T(8,128)(2,1)S(1)} %broadcast_in_dim.24), channel_id=1, replica_groups=mesh['z'=16,'c'=2,'y'=4,'x'=4] {'y','x'}, dimensions={0} | all-to-all | bytes 1966080 | tf_op jit(solution)/shard_map/all_to_all | solution.py:295
  77.5 6.7 %collective-permute-start.1 = (bf16[16,15,16,128]{3,2,1,0:T(8,128)(2,1)S(1)}, bf16[16,15,16,128]{3,2,1,0:T(8,128)(2,1)S(1)}, u32[]{:S(2)}, u32[]{:S(2)}) collective-permute-start(bf16[16,15,16,128]{3,2,1,0:T(8,128)(2,1)S(1)} %all_to_all.16.near_ref), channel_id=1, source_target_pairs={{0,16},{16,0},{1,17},{17,1},{2,18},{18,2},{3,19},{19,3},{4,20},{20... | collective-permute-start | bytes 2949128 | tf_op jit(solution)/shard_map/ppermute | solution.py:299
  84.2 0.7 reshape.66
  84.9 0.5 slice_bitcast_fusion.1
  85.4 0.9 collective-permute-done.1.far_ref
  86.3 8.4 %shard_map.119 = (bf16[5,64,1280]{2,1,0:T(8,128)(2,1)}, bf16[5,64,640]{2,1,0:T(8,128)(2,1)}, bf16[5,64,640]{2,1,0:T(8,128)(2,1)}, bf16[5,64,640]{2,1,0:T(8,128)(2,1)}) custom-call(s32[1]{0:T(128)S(6)} %copy.16.count_ref, s32[1]{0:T(128)} %bitcast.core_ref, bf16[5,64,640]{2,1,0:T(8,128)(2,1)} %q_hbm.3, bf16[5,64,640]{2,1,0:T(8,128)(2,1)} %k_hbm.3, ...), custom_call_target="tpu_custom_call" | custom-call | flops 1700000000 | bytes 8000000 | tf_op jit(solution)/shard_map/pallas_call | solution.py:265
  (17 shorter events, 0.3 us)
Async XLA Ops:
  6.3 10.8 %collective-permute-start = (bf16[208,16,128]{2,1,0:T(8,128)(2,1)S(1)}, bf16[208,16,128]{2,1,0:T(8,128)(2,1)S(1)}, u32[]{:S(2)}, u32[]{:S(2)}) collective-permute-start(bf16[208,16,128]{2,1,0:T(8,128)(2,1)S(1)} %get-tuple-element.17), channel_id=1, source_target_pairs={{0,16},{16,0},{1,17},{17,1},{2,18},{18,2},{3,19},{19,3},{4,20},{20... | collective-permute-start | bytes 2555912 | tf_op jit(solution)/shard_map/ppermute | solution.py:299
  18.2 3.8 %copy-start = (bf16[20,1280]{1,0:T(8,128)(2,1)S(1)}, bf16[20,1280]{1,0:T(8,128)(2,1)}, u32[]{:S(2)}) copy-start(bf16[20,1280]{1,0:T(8,128)(2,1)} %param.11) | copy-start | bytes 153604
  18.2 18.2 %all-to-all-start = ((bf16[16,13,16,128]{3,2,1,0:T(8,128)(2,1)}), bf16[16,13,16,128]{3,2,1,0:T(8,128)(2,1)S(1)}, u32[]{:S(2)}, u32[]{:S(2)}) async-start(bf16[16,13,16,128]{3,2,1,0:T(8,128)(2,1)} %bitcast.2), calls=%async_computation | async-start | bytes 1703936 | tf_op jit(solution)/shard_map/all_to_all | solution.py:295
  22.1 0.7 copy-start.1
  77.5 8.8 %collective-permute-start.1 = (bf16[16,15,16,128]{3,2,1,0:T(8,128)(2,1)S(1)}, bf16[16,15,16,128]{3,2,1,0:T(8,128)(2,1)S(1)}, u32[]{:S(2)}, u32[]{:S(2)}) collective-permute-start(bf16[16,15,16,128]{3,2,1,0:T(8,128)(2,1)S(1)} %all_to_all.16.near_ref), channel_id=1, source_target_pairs={{0,16},{16,0},{1,17},{17,1},{2,18},{18,2},{3,19},{19,3},{4,20},{20... | collective-permute-start | bytes 2949128 | tf_op jit(solution)/shard_map/ppermute | solution.py:299

commit v5 on v4

v5 whole, which is shorter than its diff:
```python
import jax
import jax.numpy as jnp
from jax import lax
from jax.experimental import pallas as pl
from jax.experimental.pallas import tpu as pltpu
from jax.sharding import Mesh
from jax.sharding import PartitionSpec as P

H = 8
HD = 80
WIN = 64
CAP = 5
ATTN = 640
D = 1280
Z, CORES, Y, X = 16, 2, 4, 4
SEQ = Z * CORES
HELP = Y * X
ROWS = ATTN // SEQ
BIAS = D // SEQ
HALF = ATTN // 2
BLOCKS = D // 128
PAIRS = H // 2
SPAN = 256
PART = 13
UNITS = HELP * PART
SCALE = HD**-0.5
VMEM_LIMIT = 24 * 1024 * 1024
NT = (((1,), (1,)), ((), ()))
TN = (((0,), (0,)), ((), ()))
NN = (((1,), (0,)), ((), ()))


def mm(left, right, dims):
    return lax.dot_general(left, right, dims, preferred_element_type=jnp.float32)


def head_masks(pair):
    lane = lax.broadcasted_iota(jnp.int32, (1, SPAN), 1)
    first = 32 * pair
    in_a = (lane >= first) & (lane < first + HD)
    in_b = (lane >= first + HD) & (lane < first + 2 * HD)
    return in_a.astype(jnp.float32), in_b.astype(jnp.float32)


def stacked(rows, mask_a, mask_b):
    return jnp.concatenate(
        [rows * mask_a.astype(jnp.bfloat16), rows * mask_b.astype(jnp.bfloat16)], axis=0
    )


def add_span(tiles, pair, value):
    for part in range(2):
        piece = value[:, 128 * part : 128 * (part + 1)]
        at = pair + part
        tiles[at] = piece if tiles[at] is None else tiles[at] + piece


def bias_pick():
    from_place = lax.broadcasted_iota(jnp.int32, (D, 128), 0)
    to_lane = lax.broadcasted_iota(jnp.int32, (D, 128), 1)
    owner = (from_place * 1639) >> 16
    return jnp.where(from_place - owner * BIAS == to_lane, 1.0, 0.0).astype(jnp.bfloat16)


def bias_owner(core):
    seq = lax.broadcasted_iota(jnp.int32, (Z, D), 0) * CORES + core
    place = lax.broadcasted_iota(jnp.int32, (Z, D), 1)
    return (place >= seq * BIAS) & (place < (seq + 1) * BIAS)


def row_order(core):
    place = lax.broadcasted_iota(jnp.int32, (1, HALF), 1)
    feature = (place & (Z - 1)) * (CORES * ROWS) + core * ROWS + (place >> 4)
    rows = lax.broadcasted_iota(jnp.int32, (ATTN, HALF), 0)
    return jnp.where(rows == feature, 1.0, 0.0).astype(jnp.bfloat16)


def copies(pairs, sems):
    return [
        pltpu.make_async_copy(there, here, sems.at[at]) for at, (there, here) in enumerate(pairs)
    ]


def put_units(wire_ref, made, start):
    for block in range(2):
        for row in range(ROWS):
            wire_ref[row * BLOCKS + start + block] = made[
                Z * row : Z * (row + 1), 128 * block : 128 * (block + 1)
            ].astype(jnp.bfloat16)


def put_bias(wire_ref, bias_row, core):
    owned = jnp.where(bias_owner(core), jnp.broadcast_to(bias_row, (Z, D)), 0.0)
    wire_ref[ROWS * BLOCKS] = mm(owned.astype(jnp.bfloat16), bias_pick(), NN).astype(jnp.bfloat16)
    for unit in range(ROWS * BLOCKS + 1, UNITS):
        wire_ref[unit] = jnp.zeros((Z, 128), jnp.bfloat16)


def take_units(held, weight_ref, core):
    for unit in range(ROWS * BLOCKS):
        owner, at = divmod(unit, PART)
        row, block = divmod(unit, BLOCKS)
        weight_ref[Z * row : Z * (row + 1), 128 * block : 128 * (block + 1)] = held[owner, at]
    owner, at = divmod(ROWS * BLOCKS, PART)
    spread = mm(held[owner, at], bias_pick(), NT)
    return jnp.sum(jnp.where(bias_owner(core), spread, 0.0), axis=0, keepdims=True)


def forward_kernel(
    count_ref, core_ref, q_hbm, k_hbm, v_hbm, g_hbm,
    probs_ref, att_own_ref, att_other_ref, left_ref, g_ref, bias_ref, other_ref,
    q_ref, k_ref, v_ref, natural, in_sems,
):
    count, my_core = count_ref[0], core_ref[0]
    moves = copies(((q_hbm, q_ref), (k_hbm, k_ref), (v_hbm, v_ref), (g_hbm, g_ref)), in_sems)
    for move in moves:
        move.start()
    order_own, order_other = row_order(my_core), row_order(1 - my_core)
    masks = [head_masks(pair) for pair in range(PAIRS)]
    for move in moves[:3]:
        move.wait()
    for w in range(CAP):
        rows = slice(WIN * w, WIN * (w + 1))
        tiles = [None] * (PAIRS + 1)
        for pair in range(PAIRS):
            span = slice(128 * pair, 128 * pair + SPAN)
            mask_a, mask_b = masks[pair]
            q_both = stacked(q_ref[w, :, span], mask_a, mask_b)
            scores = mm(k_ref[w, :, span], q_both, NT) * SCALE
            raised = jnp.exp(scores - jnp.max(scores, axis=0, keepdims=True))
            probs = raised * (1.0 / jnp.sum(raised, axis=0, keepdims=True))
            probs_ref[w, :, 128 * pair : 128 * (pair + 1)] = probs
            both = mm(probs.astype(jnp.bfloat16), v_ref[w, :, span], TN)
            add_span(tiles, pair, both[:WIN] * mask_a + both[WIN:] * mask_b)
        keep = jnp.where(w < count, 1.0, 0.0)
        for at, tile in enumerate(tiles):
            natural[rows, 128 * at : 128 * (at + 1)] = (tile * keep).astype(jnp.bfloat16)
    att_other = mm(natural[...], order_other, NN).astype(jnp.bfloat16)
    att_other_ref[...] = att_other
    att_own = mm(natural[...], order_own, NN).astype(jnp.bfloat16)
    att_own_ref[...] = att_own
    left_ref[...] = att_own.T
    row_of = lax.broadcasted_iota(jnp.int32, (16, CAP * WIN), 1)
    live_rows = jnp.where(row_of < count * WIN, 1.0, 0.0).astype(jnp.bfloat16)
    left = jnp.concatenate([att_other.T, live_rows], axis=0)
    moves[3].wait()
    bias_parts = []
    for start in range(0, BLOCKS, 2):
        made = mm(left, g_ref[:, 128 * start : 128 * (start + 2)], NN)
        put_units(other_ref, made, start)
        bias_parts.append(made[HALF : HALF + 1])
    bias_row = jnp.concatenate(bias_parts, axis=1)
    bias_ref[...] = bias_row
    put_bias(other_ref, bias_row, 1 - my_core)


def own_kernel(core_ref, left_ref, g_ref, bias_ref, own_ref):
    for start in range(0, BLOCKS, 2):
        put_units(own_ref, mm(left_ref[...], g_ref[:, 128 * start : 128 * (start + 2)], NN), start)
    put_bias(own_ref, bias_ref[...], core_ref[0])


def near_kernel(
    core_ref, q_hbm, k_hbm, v_hbm, g_hbm, att_own_ref, near_ref,
    q_ref, k_ref, v_ref, g_ref, first_ref, sum_ref, weight_ref, in_sems,
):
    moves = copies(((g_hbm, g_ref), (v_hbm, v_ref), (q_hbm, q_ref), (k_hbm, k_ref)), in_sems)
    for move in moves:
        move.start()
    bias = take_units(near_ref, weight_ref, core_ref[0])
    for start in range(0, D, SPAN):
        cols = slice(start, start + SPAN)
        sum_ref[:, cols] = mm(att_own_ref[...], weight_ref[:, cols], NN) + bias[:, cols]
    moves[0].wait()
    first_ref[...] = mm(g_ref[...], weight_ref[...], NT).astype(jnp.bfloat16)
    for move in moves[1:]:
        move.wait()


def backward_kernel(
    count_ref, core_ref, q_ref, k_ref, v_ref, g_ref, probs_ref, att_ref, first_ref, sum_ref,
    far_ref, enc_hbm, dq_hbm, dk_hbm, dv_hbm,
    enc_ref, dq_ref, dk_ref, dv_ref, grad_att, weight_ref, out_sems,
):
    count, my_core = count_ref[0], core_ref[0]
    masks = [head_masks(pair) for pair in range(PAIRS)]
    bias = take_units(far_ref, weight_ref, 1 - my_core)
    second = mm(g_ref[...], weight_ref[...], NT).astype(jnp.bfloat16)
    grad_att[...] = (
        mm(first_ref[...], row_order(my_core), NT) + mm(second, row_order(1 - my_core), NT)
    ).astype(jnp.bfloat16)
    live_rows = lax.broadcasted_iota(jnp.int32, (CAP * WIN, 1), 0) < count * WIN
    for w in range(CAP):
        rows = slice(WIN * w, WIN * (w + 1))
        keep = jnp.where(w < count, 1.0, 0.0)
        dq_tiles, dk_tiles, dv_tiles = ([None] * (PAIRS + 1) for _ in range(3))
        for pair in range(PAIRS):
            span = slice(128 * pair, 128 * pair + SPAN)
            mask_a, mask_b = masks[pair]
            g_both = stacked(grad_att[rows, span], mask_a, mask_b)
            q_both = stacked(q_ref[w, :, span], mask_a, mask_b)
            grad_probs = mm(v_ref[w, :, span], g_both, NT)
            probs = probs_ref[w, :, 128 * pair : 128 * (pair + 1)]
            probs_low = probs.astype(jnp.bfloat16)
            delta = jnp.sum(probs_low.astype(jnp.float32) * grad_probs, axis=0, keepdims=True)
            grad_scores = (probs * (grad_probs - delta)).astype(jnp.bfloat16)
            add_span(dv_tiles, pair, mm(probs_low, g_both, NN))
            add_span(dk_tiles, pair, mm(grad_scores, q_both, NN))
            both = mm(grad_scores, k_ref[w, :, span], TN)
            add_span(dq_tiles, pair, both[:WIN] * mask_a + both[WIN:] * mask_b)
        for at in range(PAIRS + 1):
            cols = slice(128 * at, 128 * (at + 1))
            dq_ref[w, :, cols] = (dq_tiles[at] * (keep * SCALE)).astype(jnp.bfloat16)
            dk_ref[w, :, cols] = (dk_tiles[at] * (keep * SCALE)).astype(jnp.bfloat16)
            dv_ref[w, :, cols] = (dv_tiles[at] * keep).astype(jnp.bfloat16)
        cols = slice(SPAN * w, SPAN * (w + 1))
        encoded = sum_ref[:, cols] + mm(att_ref[...], weight_ref[:, cols], NN) + bias[:, cols]
        encoded = jnp.where(live_rows, encoded, 0.0).astype(jnp.bfloat16)
        for window in range(CAP):
            enc_ref[window, :, cols] = encoded[WIN * window : WIN * (window + 1)]
    back = copies(
        ((enc_ref, enc_hbm), (dq_ref, dq_hbm), (dk_ref, dk_hbm), (dv_ref, dv_hbm)), out_sems
    )
    for move in back:
        move.start()
    for move in back:
        move.wait()


def in_hbm(value):
    return pltpu.with_memory_space_constraint(value, pltpu.HBM)


def in_vmem(value):
    return pltpu.with_memory_space_constraint(value, pltpu.VMEM)


def vmem_spec():
    return pl.BlockSpec(memory_space=pltpu.VMEM)


def hbm_spec():
    return pl.BlockSpec(memory_space=pltpu.HBM)


def smem_spec():
    return pl.BlockSpec(memory_space=pltpu.SMEM)


def call(kernel, out_shape, in_specs, out_spec, scratch_shapes, flops):
    return pl.pallas_call(
        kernel,
        out_shape=out_shape,
        in_specs=in_specs,
        out_specs=(out_spec,) * len(out_shape),
        scratch_shapes=scratch_shapes,
        compiler_params=pltpu.CompilerParams(vmem_limit_bytes=VMEM_LIMIT),
        cost_estimate=pl.CostEstimate(flops=flops, bytes_accessed=4_000_000, transcendentals=0),
    )


def forward(count, core, queries, key_rows, value_rows, grads):
    rows = pltpu.VMEM((CAP, WIN, ATTN), jnp.bfloat16)
    half = pltpu.VMEM((CAP * WIN, HALF), jnp.bfloat16)
    return call(
        forward_kernel,
        (
            pltpu.VMEM((CAP, WIN, H * WIN), jnp.float32),
            half,
            half,
            pltpu.VMEM((HALF, CAP * WIN), jnp.bfloat16),
            pltpu.VMEM((CAP * WIN, D), jnp.bfloat16),
            pltpu.VMEM((1, D), jnp.float32),
            pltpu.VMEM((UNITS, Z, 128), jnp.bfloat16),
        ),
        [smem_spec()] * 2 + [hbm_spec()] * 4,
        vmem_spec(),
        [
            rows, rows, rows, pltpu.VMEM((CAP * WIN, ATTN), jnp.bfloat16),
            pltpu.SemaphoreType.DMA((4,)),
        ],
        800_000_000,
    )(count, core, *(in_hbm(array) for array in (queries, key_rows, value_rows, grads)))


def own_half(core, left, grads, bias_row):
    return call(
        own_kernel,
        (pltpu.VMEM((UNITS, Z, 128), jnp.bfloat16),),
        [smem_spec()] + [vmem_spec()] * 3,
        vmem_spec(),
        [],
        300_000_000,
    )(core, *(in_vmem(array) for array in (left, grads, bias_row)))[0]


def near_half(core, queries, key_rows, value_rows, grads, att_own, near):
    rows = pltpu.VMEM((CAP, WIN, ATTN), jnp.bfloat16)
    return call(
        near_kernel,
        (
            rows, rows, rows, pltpu.VMEM((CAP * WIN, D), jnp.bfloat16),
            pltpu.VMEM((CAP * WIN, HALF), jnp.bfloat16), pltpu.VMEM((CAP * WIN, D), jnp.float32),
        ),
        [smem_spec()] + [hbm_spec()] * 4 + [vmem_spec()] * 2,
        vmem_spec(),
        [pltpu.VMEM((HALF, D), jnp.bfloat16), pltpu.SemaphoreType.DMA((4,))],
        600_000_000,
    )(
        core, *(in_hbm(array) for array in (queries, key_rows, value_rows, grads)),
        in_vmem(att_own), in_vmem(near),
    )


def backward(count, core, *held):
    rows = jax.ShapeDtypeStruct((CAP, WIN, ATTN), jnp.bfloat16)
    made = pltpu.VMEM((CAP, WIN, ATTN), jnp.bfloat16)
    return call(
        backward_kernel,
        (jax.ShapeDtypeStruct((CAP, WIN, D), jnp.bfloat16), rows, rows, rows),
        [smem_spec()] * 2 + [vmem_spec()] * 9,
        hbm_spec(),
        [
            pltpu.VMEM((CAP, WIN, D), jnp.bfloat16), made, made, made,
            pltpu.VMEM((CAP * WIN, ATTN), jnp.bfloat16), pltpu.VMEM((HALF, D), jnp.bfloat16),
            pltpu.SemaphoreType.DMA((4,)),
        ],
        1_200_000_000,
    )(count, core, *(in_vmem(array) for array in held))


def exchange(blocks, axis):
    return lax.all_to_all(blocks, axis, 0, 0, tiled=True)


def other_core(value):
    return lax.ppermute(value, "c", [(0, 1), (1, 0)])


def added(parts):
    return jnp.sum(parts.astype(jnp.float32), axis=0)


def own_units(proj_weight, proj_bias):
    units = jnp.concatenate(
        [
            proj_weight.reshape(ROWS * BLOCKS, 128),
            jnp.pad(proj_bias, (0, 128 - BIAS))[None],
            jnp.zeros((UNITS - ROWS * BLOCKS - 1, 128), jnp.bfloat16),
        ],
        axis=0,
    )
    mine = lax.axis_index("y") * X + lax.axis_index("x")
    return lax.dynamic_index_in_dim(units.reshape(HELP, PART, 128), mine, 0, keepdims=False)


def on_device(queries, key_rows, value_rows, grad_out, proj_weight, proj_bias, live_count):
    core = lax.axis_index("c").reshape(1)
    grads = grad_out.reshape(CAP * WIN, D)
    share = own_units(proj_weight, proj_bias)
    probs, att_own, att_other, left, held_grads, bias_row, other = forward(
        live_count, core, queries, key_rows, value_rows, grads
    )
    own = own_half(core, left, held_grads, bias_row)
    both = added(jnp.stack([own, other_core(other)])).astype(jnp.bfloat16)
    over_help = exchange(both.reshape(HELP, PART, Z, 128), ("y", "x"))
    part = added(over_help).astype(jnp.bfloat16).transpose(1, 0, 2)
    shares = jnp.broadcast_to(share[None], (Z, PART, 128))
    over_z = exchange(jnp.concatenate([part, shares], axis=1), "z")
    whole = added(over_z[:, :PART])
    high = whole.astype(jnp.bfloat16)
    low = (whole - high.astype(jnp.float32)).astype(jnp.bfloat16)
    ends = jnp.pad(jnp.stack([high, low]), ((0, 0), (0, Z - PART), (0, 0)))
    sent = jnp.concatenate([over_z[:, PART:].transpose(1, 0, 2), ends], axis=0)
    near = exchange(jnp.broadcast_to(sent[None], (HELP, PART + 2, Z, 128)), ("y", "x"))
    *held, first, partial = near_half(core, queries, key_rows, value_rows, grads, att_own, near)
    encoded, grad_queries, grad_keys, grad_values = backward(
        live_count, core, *held, probs, att_other, first, partial, other_core(near)
    )
    units = near[:, PART, :PART].astype(jnp.float32) + near[:, PART + 1, :PART].astype(jnp.float32)
    units = units.reshape(UNITS, 128)
    weight_grad = units[: ROWS * BLOCKS].reshape(ROWS, D)
    bias_grad = units[ROWS * BLOCKS, :BIAS]
    return (encoded, grad_queries, grad_keys, grad_values, weight_grad, bias_grad)


def solution(mesh):
    torus = Mesh(mesh.devices.reshape(Z, CORES, Y, X), ("z", "c", "y", "x"))
    windows = P(("z", "c", "y", "x"), None, None)
    lines, line = P(("z", "c"), None), P(("z", "c"))
    return jax.shard_map(
        on_device,
        mesh=torus,
        in_specs=(windows, windows, windows, windows, lines, line, P(("z", "c", "y", "x"))),
        out_specs=(windows, windows, windows, windows, lines, line),
        check_vma=False,
    )
```

time: 95.1 us -> 92.4 us (0.972)
  Pallas kernels: 13.4 us -> 12.4 us
  waiting for transfers between devices: 16.4 us -> 15.4 us
    ppermute x2, waiting for transfers between devices: 2.92 us -> 1.31 us  [other_core(): return lax.ppermute(value, 'c', [(0, 1), (1, 0)])]
    pallas_call x2 -> x4, Pallas kernels: 13.4 us -> 12.4 us  [the longest x1 5.84 us: backward(): call(backward_kernel, (jax.ShapeDtypeStruct((CAP, WIN, D), jnp.bfloat16),...]
  transfers between devices with their start and end apart: 3 -> 3, of which waited for: 3 -> 2; matrix products, arithmetic and copies ran while one was open for 2% -> 2% of each run, Pallas kernels for 0% -> 3%
where the time goes in v5:
time: 92.4 us; the launch traced here: 92 us
  blocking collectives  40.5 us (44%)
  starting transfers between devices  19.1 us (21%)
  waiting for transfers between devices  15.4 us (17%)
  Pallas kernels  12.4 us (13%)
  local copies, waits for them, and re-layouts  1.65 us (2%)
  between operations  1.5 us (2%)
  other arithmetic  1.49 us (2%)
    all_to_all x2, blocking collectives, exchange(): return lax.all_to_all(blocks, axis, 0, 0, tiled=True)  40.5 us
    ppermute x2, starting transfers between devices, other_core(): return lax.ppermute(value, 'c', [(0, 1), (1, 0)])  15.4 us
    all_to_all x1, waiting for transfers between devices, exchange(): return lax.all_to_all(blocks, axis, 0, 0, tiled=True)  14.1 us
    pallas_call x1, Pallas kernels, backward(): call(backward_kernel, (jax.ShapeDtypeStruct((CAP, WIN, D), jnp.bfloat16),...  5.84 us
    pallas_call x1, Pallas kernels, forward(): call(forward_kernel, (pltpu.VMEM((CAP, WIN, H * WIN), jnp.float32), half,...  4.1 us
    all_to_all x1, starting transfers between devices, exchange(): return lax.all_to_all(blocks, axis, 0, 0, tiled=True)  3.62 us
  transfers between devices with their start and end apart: 3, of which 2 were waited for; matrix products, arithmetic and copies ran while one was open for 2% of the time, Pallas kernels for 3%

profile of v5, /device:TPU:1, one launch (start us, length us, event | category | flops | bytes accessed | tf_op | source)
XLA Modules:
  0.0 92.0 jit_solution(11109612573769724161)
XLA Ops:
  1.3 4.1 %shard_map.118 = (f32[5,64,512]{2,1,0:T(8,128)S(1)}, bf16[320,320]{1,0:T(8,128)(2,1)S(1)}, bf16[320,320]{1,0:T(8,128)(2,1)S(1)}, bf16[320,320]{1,0:T(8,128)(2,1)...) custom-call(s32[1]{0:T(128)S(6)} %copy.16.count_ref, ...), custom_call_target="tpu_custom_call" | custom-call | flops 800000000 | bytes 4000000 | tf_op jit(solution)/shard_map/pallas_call | solution.py:265
  5.4 8.8 %collective-permute-start = (bf16[208,16,128]{2,1,0:T(8,128)(2,1)S(1)}, bf16[208,16,128]{2,1,0:T(8,128)(2,1)S(1)}, u32[]{:S(2)}, u32[]{:S(2)}) collective-permute-start(bf16[208,16,128]{2,1,0:T(8,128)(2,1)S(1)} %get-tuple-element.27), channel_id=1, source_target_pairs={{0,16},{16,0},{1,17},{17,1},{2,18},{18,2},{3,19},{19,3},{4,20},{20... | collective-permute-start | bytes 2555912 | tf_op jit(solution)/shard_map/ppermute | solution.py:337
  14.2 0.6 shard_map.119
  14.8 0.0 copy-start
  14.8 0.0 copy-start.1
  14.9 1.3 %collective-permute-done = bf16[208,16,128]{2,1,0:T(8,128)(2,1)S(1)} collective-permute-done((bf16[208,16,128]{2,1,0:T(8,128)(2,1)S(1)}, bf16[208,16,128]{2,1,0:T(8,128)(2,1)S(1)}, u32[]{:S(2)}, u32[]{:S(2)}) %collective-permute-start) | collective-permute-done | bytes 852000 | tf_op jit(solution)/shard_map/ppermute | solution.py:337
  16.2 1.2 %reduce_sum.33 = bf16[208,16,128]{2,1,0:T(8,128)(2,1)} add(bf16[208,16,128]{2,1,0:T(8,128)(2,1)S(1)} %shard_map.119, bf16[208,16,128]{2,1,0:T(8,128)(2,1)S(1)} %collective-permute-done) | non-fusion elementwise | flops 425984 | bytes 2555904 | tf_op jit(solution)/shard_map/reduce_sum | solution.py:341
  17.3 3.6 %all-to-all-start = ((bf16[16,13,16,128]{3,2,1,0:T(8,128)(2,1)}), bf16[16,13,16,128]{3,2,1,0:T(8,128)(2,1)S(1)}, u32[]{:S(2)}, u32[]{:S(2)}) async-start(bf16[16,13,16,128]{3,2,1,0:T(8,128)(2,1)} %bitcast.2), calls=%async_computation | async-start | bytes 1703936 | tf_op jit(solution)/shard_map/all_to_all | solution.py:333
  21.0 0.0 copy-done
  21.0 0.1 reshape.64
  21.1 0.1 pad.18.clone
  21.2 0.0 copy-done.1
  21.2 0.1 maximum_maximum_fusion
  21.3 14.1 %all-to-all-done = bf16[16,13,16,128]{3,2,1,0:T(8,128)(2,1)S(1)} async-done(((bf16[16,13,16,128]{3,2,1,0:T(8,128)(2,1)}), bf16[16,13,16,128]{3,2,1,0:T(8,128)(2,1)S(1)}, u32[]{:S(2)}, u32[]{:S(2)}) %all-to-all-start) | async-done | bytes 852000 | tf_op jit(solution)/shard_map/all_to_all | solution.py:333
  35.4 0.1 reduce_sum.34
  35.6 24.2 %all_to_all.15 = bf16[16,26,128]{2,1,0:T(8,128)(2,1)S(1)} all-to-all(bf16[16,26,128]{2,1,0:T(8,128)(2,1)S(1)} %copy.14), channel_id=1, replica_groups=mesh['z'=16,'c'=2,'y'=4,'x'=4] {'z'}, dimensions={0} | all-to-all | bytes 212992 | tf_op jit(solution)/shard_map/all_to_all | solution.py:333
  60.0 0.1 broadcast_in_dim.24
  60.2 16.3 %all_to_all.16.near_ref = bf16[16,15,16,128]{3,2,1,0:T(8,128)(2,1)S(1)} all-to-all(bf16[16,15,16,128]{3,2,1,0:T(8,128)(2,1)S(1)} %broadcast_in_dim.24), channel_id=1, replica_groups=mesh['z'=16,'c'=2,'y'=4,'x'=4] {'y','x'}, dimensions={0} | all-to-all | bytes 1966080 | tf_op jit(solution)/shard_map/all_to_all | solution.py:333
  76.5 6.7 %collective-permute-start.1 = (bf16[16,15,16,128]{3,2,1,0:T(8,128)(2,1)S(1)}, bf16[16,15,16,128]{3,2,1,0:T(8,128)(2,1)S(1)}, u32[]{:S(2)}, u32[]{:S(2)}) collective-permute-start(bf16[16,15,16,128]{3,2,1,0:T(8,128)(2,1)S(1)} %all_to_all.16.near_ref), channel_id=1, source_target_pairs={{0,16},{16,0},{1,17},{17,1},{2,18},{18,2},{3,19},{19,3},{4,20},{20... | collective-permute-start | bytes 2949128 | tf_op jit(solution)/shard_map/ppermute | solution.py:337
  83.2 0.7 reshape.66
  83.9 1.8 %shard_map.120 = (bf16[5,64,640]{2,1,0:T(8,128)(2,1)S(1)}, bf16[5,64,640]{2,1,0:T(8,128)(2,1)S(1)}, bf16[5,64,640]{2,1,0:T(8,128)(2,1)S(1)}, bf16[320,1280]{1,0:...) custom-call(s32[1]{0:T(128)} %bitcast.core_ref, bf16[5,64,640]{2,1,0:T(8,128)(2,1)} %q_hbm.3, ...), custom_call_target="tpu_custom_call" | custom-call | flops 600000000 | bytes 4000000 | tf_op jit(solution)/shard_map/pallas_call | solution.py:299
  85.7 0.5 slice_bitcast_fusion.1
  86.2 0.0 collective-permute-done.1.far_ref
  86.2 5.8 %shard_map.121 = (bf16[5,64,1280]{2,1,0:T(8,128)(2,1)}, bf16[5,64,640]{2,1,0:T(8,128)(2,1)}, bf16[5,64,640]{2,1,0:T(8,128)(2,1)}, bf16[5,64,640]{2,1,0:T(8,128)(2,1)}) custom-call(s32[1]{0:T(128)S(6)} %copy.16.count_ref, s32[1]{0:T(128)} %bitcast.core_ref, bf16[5,64,640]{2,1,0:T(8,128)(2,1)S(1)} %get-tuple-element.28.q_ref, ...), custom_call_target="tpu_custom_call" | custom-call | flops 1200000000 | bytes 4000000 | tf_op jit(solution)/shard_map/pallas_call | solution.py:318
  (17 shorter events, 0.3 us)
Async XLA Ops:
  5.4 10.8 %collective-permute-start = (bf16[208,16,128]{2,1,0:T(8,128)(2,1)S(1)}, bf16[208,16,128]{2,1,0:T(8,128)(2,1)S(1)}, u32[]{:S(2)}, u32[]{:S(2)}) collective-permute-start(bf16[208,16,128]{2,1,0:T(8,128)(2,1)S(1)} %get-tuple-element.27), channel_id=1, source_target_pairs={{0,16},{16,0},{1,17},{17,1},{2,18},{18,2},{3,19},{19,3},{4,20},{20... | collective-permute-start | bytes 2555912 | tf_op jit(solution)/shard_map/ppermute | solution.py:337
  14.8 6.1 %copy-start = (bf16[20,1280]{1,0:T(8,128)(2,1)S(1)}, bf16[20,1280]{1,0:T(8,128)(2,1)}, u32[]{:S(2)}) copy-start(bf16[20,1280]{1,0:T(8,128)(2,1)} %param.11) | copy-start | bytes 153604
  14.8 6.3 %copy-start.1 = (bf16[40]{0:T(256)(128)(2,1)S(1)}, bf16[40]{0:T(256)(128)(2,1)}, u32[]{:S(2)}) copy-start(bf16[40]{0:T(256)(128)(2,1)} %param.12) | copy-start | bytes 244
  17.3 18.1 %all-to-all-start = ((bf16[16,13,16,128]{3,2,1,0:T(8,128)(2,1)}), bf16[16,13,16,128]{3,2,1,0:T(8,128)(2,1)S(1)}, u32[]{:S(2)}, u32[]{:S(2)}) async-start(bf16[16,13,16,128]{3,2,1,0:T(8,128)(2,1)} %bitcast.2), calls=%async_computation | async-start | bytes 1703936 | tf_op jit(solution)/shard_map/all_to_all | solution.py:333
  76.5 9.7 %collective-permute-start.1 = (bf16[16,15,16,128]{3,2,1,0:T(8,128)(2,1)S(1)}, bf16[16,15,16,128]{3,2,1,0:T(8,128)(2,1)S(1)}, u32[]{:S(2)}, u32[]{:S(2)}) collective-permute-start(bf16[16,15,16,128]{3,2,1,0:T(8,128)(2,1)S(1)} %all_to_all.16.near_ref), channel_id=1, source_target_pairs={{0,16},{16,0},{1,17},{17,1},{2,18},{18,2},{3,19},{19,3},{4,20},{20... | collective-permute-start | bytes 2949128 | tf_op jit(solution)/shard_map/ppermute | solution.py:337

commit v6 on v5

--- a/solution.py
+++ b/solution.py
@@ -108,14 +108,14 @@
 
 def forward_kernel(
     count_ref, core_ref, q_hbm, k_hbm, v_hbm, g_hbm,
-    probs_ref, att_own_ref, att_other_ref, left_ref, g_ref, bias_ref, other_ref,
-    q_ref, k_ref, v_ref, natural, in_sems,
+    probs_ref, natural, att_other_ref, g_ref, bias_ref, other_ref,
+    q_ref, k_ref, v_ref, in_sems,
 ):
     count, my_core = count_ref[0], core_ref[0]
     moves = copies(((q_hbm, q_ref), (k_hbm, k_ref), (v_hbm, v_ref), (g_hbm, g_ref)), in_sems)
     for move in moves:
         move.start()
-    order_own, order_other = row_order(my_core), row_order(1 - my_core)
+    order_other = row_order(1 - my_core)
     masks = [head_masks(pair) for pair in range(PAIRS)]
     for move in moves[:3]:
         move.wait()
@@ -137,9 +137,6 @@
             natural[rows, 128 * at : 128 * (at + 1)] = (tile * keep).astype(jnp.bfloat16)
     att_other = mm(natural[...], order_other, NN).astype(jnp.bfloat16)
     att_other_ref[...] = att_other
-    att_own = mm(natural[...], order_own, NN).astype(jnp.bfloat16)
-    att_own_ref[...] = att_own
-    left_ref[...] = att_own.T
     row_of = lax.broadcasted_iota(jnp.int32, (16, CAP * WIN), 1)
     live_rows = jnp.where(row_of < count * WIN, 1.0, 0.0).astype(jnp.bfloat16)
     left = jnp.concatenate([att_other.T, live_rows], axis=0)
@@ -154,19 +151,31 @@
     put_bias(other_ref, bias_row, 1 - my_core)
 
 
-def own_kernel(core_ref, left_ref, g_ref, bias_ref, own_ref):
+def own_kernel(core_ref, natural, g_ref, bias_ref, own_ref, att_own_ref):
+    att_own = mm(natural[...], row_order(core_ref[0]), NN).astype(jnp.bfloat16)
+    att_own_ref[...] = att_own
+    left = att_own.T
     for start in range(0, BLOCKS, 2):
-        put_units(own_ref, mm(left_ref[...], g_ref[:, 128 * start : 128 * (start + 2)], NN), start)
+        put_units(own_ref, mm(left, g_ref[:, 128 * start : 128 * (start + 2)], NN), start)
     put_bias(own_ref, bias_ref[...], core_ref[0])
 
 
 def near_kernel(
     core_ref, q_hbm, k_hbm, v_hbm, g_hbm, att_own_ref, near_ref,
-    q_ref, k_ref, v_ref, g_ref, first_ref, sum_ref, weight_ref, in_sems,
+    q_ref, k_ref, v_ref, g_ref, first_ref, sum_ref, grad_hbm, weight_ref, grad_ref, in_sems,
+    out_sem,
 ):
     moves = copies(((g_hbm, g_ref), (v_hbm, v_ref), (q_hbm, q_ref), (k_hbm, k_ref)), in_sems)
     for move in moves:
         move.start()
+    for owner in range(HELP):
+        made = near_ref[owner, PART].astype(jnp.float32)
+        for at in range(PART):
+            row, block = divmod(owner * PART + at, BLOCKS)
+            if row < ROWS:
+                grad_ref[row : row + 1, 128 * block : 128 * (block + 1)] = made[at : at + 1]
+    grad_move = pltpu.make_async_copy(grad_ref, grad_hbm, out_sem)
+    grad_move.start()
     bias = take_units(near_ref, weight_ref, core_ref[0])
     for start in range(0, D, SPAN):
         cols = slice(start, start + SPAN)
@@ -175,6 +184,7 @@
     first_ref[...] = mm(g_ref[...], weight_ref[...], NT).astype(jnp.bfloat16)
     for move in moves[1:]:
         move.wait()
+    grad_move.wait()
 
 
 def backward_kernel(
@@ -247,12 +257,12 @@
     return pl.BlockSpec(memory_space=pltpu.SMEM)
 
 
-def call(kernel, out_shape, in_specs, out_spec, scratch_shapes, flops):
+def call(kernel, out_shape, in_specs, out_specs, scratch_shapes, flops):
     return pl.pallas_call(
         kernel,
         out_shape=out_shape,
         in_specs=in_specs,
-        out_specs=(out_spec,) * len(out_shape),
+        out_specs=out_specs,
         scratch_shapes=scratch_shapes,
         compiler_params=pltpu.CompilerParams(vmem_limit_bytes=VMEM_LIMIT),
         cost_estimate=pl.CostEstimate(flops=flops, bytes_accessed=4_000_000, transcendentals=0),
@@ -261,37 +271,37 @@
 
 def forward(count, core, queries, key_rows, value_rows, grads):
     rows = pltpu.VMEM((CAP, WIN, ATTN), jnp.bfloat16)
-    half = pltpu.VMEM((CAP * WIN, HALF), jnp.bfloat16)
     return call(
         forward_kernel,
         (
             pltpu.VMEM((CAP, WIN, H * WIN), jnp.float32),
-            half,
-            half,
-            pltpu.VMEM((HALF, CAP * WIN), jnp.bfloat16),
+            pltpu.VMEM((CAP * WIN, ATTN), jnp.bfloat16),
+            pltpu.VMEM((CAP * WIN, HALF), jnp.bfloat16),
             pltpu.VMEM((CAP * WIN, D), jnp.bfloat16),
             pltpu.VMEM((1, D), jnp.float32),
             pltpu.VMEM((UNITS, Z, 128), jnp.bfloat16),
         ),
         [smem_spec()] * 2 + [hbm_spec()] * 4,
-        vmem_spec(),
+        (vmem_spec(),) * 6,
         [
-            rows, rows, rows, pltpu.VMEM((CAP * WIN, ATTN), jnp.bfloat16),
-            pltpu.SemaphoreType.DMA((4,)),
+            rows, rows, rows, pltpu.SemaphoreType.DMA((4,)),
         ],
         800_000_000,
     )(count, core, *(in_hbm(array) for array in (queries, key_rows, value_rows, grads)))
 
 
-def own_half(core, left, grads, bias_row):
+def own_half(core, attended, grads, bias_row):
     return call(
         own_kernel,
-        (pltpu.VMEM((UNITS, Z, 128), jnp.bfloat16),),
+        (
+            pltpu.VMEM((UNITS, Z, 128), jnp.bfloat16),
+            pltpu.VMEM((CAP * WIN, HALF), jnp.bfloat16),
+        ),
         [smem_spec()] + [vmem_spec()] * 3,
-        vmem_spec(),
+        (vmem_spec(),) * 2,
         [],
         300_000_000,
-    )(core, *(in_vmem(array) for array in (left, grads, bias_row)))[0]
+    )(core, *(in_vmem(array) for array in (attended, grads, bias_row)))
 
 
 def near_half(core, queries, key_rows, value_rows, grads, att_own, near):
@@ -301,10 +311,14 @@
         (
             rows, rows, rows, pltpu.VMEM((CAP * WIN, D), jnp.bfloat16),
             pltpu.VMEM((CAP * WIN, HALF), jnp.bfloat16), pltpu.VMEM((CAP * WIN, D), jnp.float32),
+            jax.ShapeDtypeStruct((ROWS, D), jnp.float32),
         ),
         [smem_spec()] + [hbm_spec()] * 4 + [vmem_spec()] * 2,
-        vmem_spec(),
-        [pltpu.VMEM((HALF, D), jnp.bfloat16), pltpu.SemaphoreType.DMA((4,))],
+        (vmem_spec(),) * 6 + (hbm_spec(),),
+        [
+            pltpu.VMEM((HALF, D), jnp.bfloat16), pltpu.VMEM((ROWS, D), jnp.float32),
+            pltpu.SemaphoreType.DMA((4,)), pltpu.SemaphoreType.DMA,
+        ],
         600_000_000,
     )(
         core, *(in_hbm(array) for array in (queries, key_rows, value_rows, grads)),
@@ -319,7 +333,7 @@
         backward_kernel,
         (jax.ShapeDtypeStruct((CAP, WIN, D), jnp.bfloat16), rows, rows, rows),
         [smem_spec()] * 2 + [vmem_spec()] * 9,
-        hbm_spec(),
+        (hbm_spec(),) * 4,
         [
             pltpu.VMEM((CAP, WIN, D), jnp.bfloat16), made, made, made,
             pltpu.VMEM((CAP * WIN, ATTN), jnp.bfloat16), pltpu.VMEM((HALF, D), jnp.bfloat16),
@@ -358,29 +372,27 @@
     core = lax.axis_index("c").reshape(1)
     grads = grad_out.reshape(CAP * WIN, D)
     share = own_units(proj_weight, proj_bias)
-    probs, att_own, att_other, left, held_grads, bias_row, other = forward(
+    probs, attended, att_other, held_grads, bias_row, other = forward(
         live_count, core, queries, key_rows, value_rows, grads
     )
-    own = own_half(core, left, held_grads, bias_row)
+    own, att_own = own_half(core, attended, held_grads, bias_row)
     both = added(jnp.stack([own, other_core(other)])).astype(jnp.bfloat16)
     over_help = exchange(both.reshape(HELP, PART, Z, 128), ("y", "x"))
     part = added(over_help).astype(jnp.bfloat16).transpose(1, 0, 2)
     shares = jnp.broadcast_to(share[None], (Z, PART, 128))
     over_z = exchange(jnp.concatenate([part, shares], axis=1), "z")
     whole = added(over_z[:, :PART])
-    high = whole.astype(jnp.bfloat16)
-    low = (whole - high.astype(jnp.float32)).astype(jnp.bfloat16)
-    ends = jnp.pad(jnp.stack([high, low]), ((0, 0), (0, Z - PART), (0, 0)))
+    ends = jnp.pad(whole.astype(jnp.bfloat16), ((0, Z - PART), (0, 0)))[None]
     sent = jnp.concatenate([over_z[:, PART:].transpose(1, 0, 2), ends], axis=0)
-    near = exchange(jnp.broadcast_to(sent[None], (HELP, PART + 2, Z, 128)), ("y", "x"))
-    *held, first, partial = near_half(core, queries, key_rows, value_rows, grads, att_own, near)
+    near = exchange(jnp.broadcast_to(sent[None], (HELP, PART + 1, Z, 128)), ("y", "x"))
+    *held, first, partial, weight_grad = near_half(
+        core, queries, key_rows, value_rows, grads, att_own, near
+    )
     encoded, grad_queries, grad_keys, grad_values = backward(
         live_count, core, *held, probs, att_other, first, partial, other_core(near)
     )
-    units = near[:, PART, :PART].astype(jnp.float32) + near[:, PART + 1, :PART].astype(jnp.float32)
-    units = units.reshape(UNITS, 128)
-    weight_grad = units[: ROWS * BLOCKS].reshape(ROWS, D)
-    bias_grad = units[ROWS * BLOCKS, :BIAS]
+    owner, at = divmod(ROWS * BLOCKS, PART)
+    bias_grad = near[owner, PART, at, :BIAS].astype(jnp.float32)
     return (encoded, grad_queries, grad_keys, grad_values, weight_grad, bias_grad)
 
 

time: 92.4 us -> 91 us (0.985)
  local copies, waits for them, and re-layouts: 1.65 us -> 0.42 us
  transfers between devices with their start and end apart: 3 -> 3, of which waited for: 2 -> 2; matrix products, arithmetic and copies ran while one was open for 2% -> 1% of each run, Pallas kernels for 3% -> 3%
where the time goes in v6:
time: 91 us; the launch traced here: 90.7 us
  blocking collectives  40 us (44%)
  starting transfers between devices  18.9 us (21%)
  waiting for transfers between devices  15 us (16%)
  Pallas kernels  13 us (14%)
  other arithmetic  1.93 us (2%)
  between operations  1.45 us (2%)
    all_to_all x2, blocking collectives, exchange(): return lax.all_to_all(blocks, axis, 0, 0, tiled=True)  40 us
    ppermute x2, starting transfers between devices, other_core(): return lax.ppermute(value, 'c', [(0, 1), (1, 0)])  15.3 us
    all_to_all x1, waiting for transfers between devices, exchange(): return lax.all_to_all(blocks, axis, 0, 0, tiled=True)  14.1 us
    pallas_call x1, Pallas kernels, backward(): call(backward_kernel, (jax.ShapeDtypeStruct((CAP, WIN, D), jnp.bfloat16),...  5.85 us
    pallas_call x1, Pallas kernels, forward(): call(forward_kernel, (pltpu.VMEM((CAP, WIN, H * WIN), jnp.float32), pltpu...  4.24 us
    all_to_all x1, starting transfers between devices, exchange(): return lax.all_to_all(blocks, axis, 0, 0, tiled=True)  3.62 us
  transfers between devices with their start and end apart: 3, of which 2 were waited for; matrix products, arithmetic and copies ran while one was open for 1% of the time, Pallas kernels for 3%

profile of v6, /device:TPU:1, one launch (start us, length us, event | category | flops | bytes accessed | tf_op | source)
XLA Modules:
  0.0 90.7 jit_solution(4686059045794491938)
XLA Ops:
  1.3 4.2 %shard_map.118 = (f32[5,64,512]{2,1,0:T(8,128)S(1)}, bf16[320,640]{1,0:T(8,128)(2,1)S(1)}, bf16[320,320]{1,0:T(8,128)(2,1)S(1)}, bf16[320,1280]{1,0:T(8,128)(2,1...) custom-call(s32[1]{0:T(128)S(6)} %copy.19.count_ref, s32[1]{0:T(128)} %bitcast.core_ref, ...), custom_call_target="tpu_custom_call" | custom-call | flops 800000000 | bytes 4000000 | tf_op jit(solution)/shard_map/pallas_call | solution.py:274
  5.5 8.8 %collective-permute-start = (bf16[208,16,128]{2,1,0:T(8,128)(2,1)S(1)}, bf16[208,16,128]{2,1,0:T(8,128)(2,1)S(1)}, u32[]{:S(2)}, u32[]{:S(2)}) collective-permute-start(bf16[208,16,128]{2,1,0:T(8,128)(2,1)S(1)} %get-tuple-element.30), channel_id=1, source_target_pairs={{0,16},{16,0},{1,17},{17,1},{2,18},{18,2},{3,19},{19,3},{4,20},{20... | collective-permute-start | bytes 2555912 | tf_op jit(solution)/shard_map/ppermute | solution.py:351
  14.3 1.1 %shard_map.119 = (bf16[208,16,128]{2,1,0:T(8,128)(2,1)S(1)}, bf16[320,320]{1,0:T(8,128)(2,1)S(1)}) custom-call(s32[1]{0:T(128)} %bitcast.core_ref, bf16[320,640]{1,0:T(8,128)(2,1)S(1)} %get-tuple-element.25.natural, bf16[320,1280]{1,0:T(8,128)(2,1)S(1)} %get-tuple-element.26.g_ref, f32[1,1280]{1,0:T(1,128)S(1)} %get-tuple-element.27.bias_ref), custom_call_target="tpu_custom_call" | custom-call | flops 300000000 | bytes 4000000 | tf_op jit(solution)/shard_map/pallas_call | solution.py:294
  15.4 0.9 collective-permute-done
  16.3 0.0 copy-start
  16.3 0.0 copy-start.1
  16.3 1.1 %reduce_sum.34 = bf16[208,16,128]{2,1,0:T(8,128)(2,1)} add(bf16[208,16,128]{2,1,0:T(8,128)(2,1)S(1)} %get-tuple-element.29, bf16[208,16,128]{2,1,0:T(8,128)(2,1)S(1)} %collective-permute-done) | non-fusion elementwise | flops 425984 | bytes 2555904 | tf_op jit(solution)/shard_map/reduce_sum | solution.py:355
  17.4 3.6 %all-to-all-start = ((bf16[16,13,16,128]{3,2,1,0:T(8,128)(2,1)}), bf16[16,13,16,128]{3,2,1,0:T(8,128)(2,1)S(1)}, u32[]{:S(2)}, u32[]{:S(2)}) async-start(bf16[16,13,16,128]{3,2,1,0:T(8,128)(2,1)} %bitcast.2), calls=%async_computation | async-start | bytes 1703936 | tf_op jit(solution)/shard_map/all_to_all | solution.py:347
  21.1 0.0 copy-done
  21.1 0.1 reshape.37
  21.2 0.1 pad.16.clone
  21.3 0.0 copy-done.1
  21.3 0.1 maximum_maximum_fusion
  21.4 14.1 %all-to-all-done = bf16[16,13,16,128]{3,2,1,0:T(8,128)(2,1)S(1)} async-done(((bf16[16,13,16,128]{3,2,1,0:T(8,128)(2,1)}), bf16[16,13,16,128]{3,2,1,0:T(8,128)(2,1)S(1)}, u32[]{:S(2)}, u32[]{:S(2)}) %all-to-all-start) | async-done | bytes 852000 | tf_op jit(solution)/shard_map/all_to_all | solution.py:347
  35.5 0.1 reduce_sum.35
  35.7 24.2 %all_to_all.15 = bf16[16,26,128]{2,1,0:T(8,128)(2,1)S(1)} all-to-all(bf16[16,26,128]{2,1,0:T(8,128)(2,1)S(1)} %copy.16), channel_id=1, replica_groups=mesh['z'=16,'c'=2,'y'=4,'x'=4] {'z'}, dimensions={0} | all-to-all | bytes 212992 | tf_op jit(solution)/shard_map/all_to_all | solution.py:347
  60.1 0.1 broadcast_in_dim.28
  60.2 15.8 %all_to_all.16.near_ref = bf16[16,14,16,128]{3,2,1,0:T(8,128)(2,1)S(1)} all-to-all(bf16[16,14,16,128]{3,2,1,0:T(8,128)(2,1)S(1)} %broadcast_in_dim.28), channel_id=1, replica_groups=mesh['z'=16,'c'=2,'y'=4,'x'=4] {'y','x'}, dimensions={0} | all-to-all | bytes 1835008 | tf_op jit(solution)/shard_map/all_to_all | solution.py:347
  76.0 6.5 %collective-permute-start.1 = (bf16[16,14,16,128]{3,2,1,0:T(8,128)(2,1)S(1)}, bf16[16,14,16,128]{3,2,1,0:T(8,128)(2,1)S(1)}, u32[]{:S(2)}, u32[]{:S(2)}) collective-permute-start(bf16[16,14,16,128]{3,2,1,0:T(8,128)(2,1)S(1)} %all_to_all.16.near_ref), channel_id=1, source_target_pairs={{0,16},{16,0},{1,17},{17,1},{2,18},{18,2},{3,19},{19,3},{4,20},{20... | collective-permute-start | bytes 2752520 | tf_op jit(solution)/shard_map/ppermute | solution.py:351
  82.5 1.8 %shard_map.120 = (bf16[5,64,640]{2,1,0:T(8,128)(2,1)S(1)}, bf16[5,64,640]{2,1,0:T(8,128)(2,1)S(1)}, bf16[5,64,640]{2,1,0:T(8,128)(2,1)S(1)}, bf16[320,1280]{1,0:...) custom-call(s32[1]{0:T(128)} %bitcast.core_ref, ...), custom_call_target="tpu_custom_call" | custom-call | flops 600000000 | bytes 4000000 | tf_op jit(solution)/shard_map/pallas_call | solution.py:309
  84.3 0.5 fusion
  84.8 0.0 collective-permute-done.1.far_ref
  84.8 5.8 %shard_map.121 = (bf16[5,64,1280]{2,1,0:T(8,128)(2,1)}, bf16[5,64,640]{2,1,0:T(8,128)(2,1)}, bf16[5,64,640]{2,1,0:T(8,128)(2,1)}, bf16[5,64,640]{2,1,0:T(8,128)(2,1)}) custom-call(s32[1]{0:T(128)S(6)} %copy.19.count_ref, s32[1]{0:T(128)} %bitcast.core_ref, bf16[5,64,640]{2,1,0:T(8,128)(2,1)S(1)} %get-tuple-element.31.q_ref, ...), custom_call_target="tpu_custom_call" | custom-call | flops 1200000000 | bytes 4000000 | tf_op jit(solution)/shard_map/pallas_call | solution.py:332
  (12 shorter events, 0.2 us)
Async XLA Ops:
  5.5 10.8 %collective-permute-start = (bf16[208,16,128]{2,1,0:T(8,128)(2,1)S(1)}, bf16[208,16,128]{2,1,0:T(8,128)(2,1)S(1)}, u32[]{:S(2)}, u32[]{:S(2)}) collective-permute-start(bf16[208,16,128]{2,1,0:T(8,128)(2,1)S(1)} %get-tuple-element.30), channel_id=1, source_target_pairs={{0,16},{16,0},{1,17},{17,1},{2,18},{18,2},{3,19},{19,3},{4,20},{20... | collective-permute-start | bytes 2555912 | tf_op jit(solution)/shard_map/ppermute | solution.py:351
  16.3 4.8 %copy-start = (bf16[20,1280]{1,0:T(8,128)(2,1)S(1)}, bf16[20,1280]{1,0:T(8,128)(2,1)}, u32[]{:S(2)}) copy-start(bf16[20,1280]{1,0:T(8,128)(2,1)} %param.11) | copy-start | bytes 153604
  16.3 5.0 %copy-start.1 = (bf16[40]{0:T(256)(128)(2,1)S(1)}, bf16[40]{0:T(256)(128)(2,1)}, u32[]{:S(2)}) copy-start(bf16[40]{0:T(256)(128)(2,1)} %param.12) | copy-start | bytes 244
  17.4 18.1 %all-to-all-start = ((bf16[16,13,16,128]{3,2,1,0:T(8,128)(2,1)}), bf16[16,13,16,128]{3,2,1,0:T(8,128)(2,1)S(1)}, u32[]{:S(2)}, u32[]{:S(2)}) async-start(bf16[16,13,16,128]{3,2,1,0:T(8,128)(2,1)} %bitcast.2), calls=%async_computation | async-start | bytes 1703936 | tf_op jit(solution)/shard_map/all_to_all | solution.py:347
  76.0 8.8 %collective-permute-start.1 = (bf16[16,14,16,128]{3,2,1,0:T(8,128)(2,1)S(1)}, bf16[16,14,16,128]{3,2,1,0:T(8,128)(2,1)S(1)}, u32[]{:S(2)}, u32[]{:S(2)}) collective-permute-start(bf16[16,14,16,128]{3,2,1,0:T(8,128)(2,1)S(1)} %all_to_all.16.near_ref), channel_id=1, source_target_pairs={{0,16},{16,0},{1,17},{17,1},{2,18},{18,2},{3,19},{19,3},{4,20},{20... | collective-permute-start | bytes 2752520 | tf_op jit(solution)/shard_map/ppermute | solution.py:351

commit v7 on v6

--- a/solution.py
+++ b/solution.py
@@ -377,9 +377,9 @@
     )
     own, att_own = own_half(core, attended, held_grads, bias_row)
     both = added(jnp.stack([own, other_core(other)])).astype(jnp.bfloat16)
+    both, shares = lax.optimization_barrier((both, jnp.broadcast_to(share[None], (Z, PART, 128))))
     over_help = exchange(both.reshape(HELP, PART, Z, 128), ("y", "x"))
     part = added(over_help).astype(jnp.bfloat16).transpose(1, 0, 2)
-    shares = jnp.broadcast_to(share[None], (Z, PART, 128))
     over_z = exchange(jnp.concatenate([part, shares], axis=1), "z")
     whole = added(over_z[:, :PART])
     ends = jnp.pad(whole.astype(jnp.bfloat16), ((0, Z - PART), (0, 0)))[None]

time: 91 us -> 91.1 us (level)
  blocking collectives: 40 us -> 57.8 us
  waiting for transfers between devices: 15 us -> 0.63 us
  starting transfers between devices: 18.9 us -> 15.2 us
    all_to_all x2 -> x3, blocking collectives: 40 us -> 57.8 us  [exchange(): return lax.all_to_all(blocks, axis, 0, 0, tiled=True)]
    all_to_all x1 -> x0, waiting for transfers between devices: 14.1 us -> none  [exchange(): return lax.all_to_all(blocks, axis, 0, 0, tiled=True)]
    all_to_all x1 -> x0, starting transfers between devices: 3.62 us -> none  [exchange(): return lax.all_to_all(blocks, axis, 0, 0, tiled=True)]
  transfers between devices with their start and end apart: 3 -> 2, of which waited for: 2 -> 1; matrix products, arithmetic and copies ran while one was open for 1% -> 1% of each run, Pallas kernels for 3% -> 3%
where the time goes in v7:
time: 91.1 us; the launch traced here: 90.7 us
  blocking collectives  57.8 us (63%)
  starting transfers between devices  15.2 us (17%)
  Pallas kernels  13 us (14%)
  other arithmetic  2.18 us (2%)
  between operations  1.48 us (2%)
    all_to_all x3, blocking collectives, exchange(): return lax.all_to_all(blocks, axis, 0, 0, tiled=True)  57.8 us
    ppermute x2, starting transfers between devices, other_core(): return lax.ppermute(value, 'c', [(0, 1), (1, 0)])  15.2 us
    pallas_call x1, Pallas kernels, backward(): call(backward_kernel, (jax.ShapeDtypeStruct((CAP, WIN, D), jnp.bfloat16),...  5.85 us
    pallas_call x1, Pallas kernels, forward(): call(forward_kernel, (pltpu.VMEM((CAP, WIN, H * WIN), jnp.float32), pltpu...  4.24 us
  transfers between devices with their start and end apart: 2, of which 1 were waited for; matrix products, arithmetic and copies ran while one was open for 1% of the time, Pallas kernels for 3%

profile of v7, /device:TPU:1, one launch (start us, length us, event | category | flops | bytes accessed | tf_op | source)
XLA Modules:
  0.0 90.7 jit_solution(16532779071275414431)
XLA Ops:
  0.6 0.0 copy-start
  0.6 0.0 copy-start.1
  1.3 4.2 %shard_map.118 = (f32[5,64,512]{2,1,0:T(8,128)S(1)}, bf16[320,640]{1,0:T(8,128)(2,1)S(1)}, bf16[320,320]{1,0:T(8,128)(2,1)S(1)}, bf16[320,1280]{1,0:T(8,128)(2,1...) custom-call(s32[1]{0:T(128)S(6)} %copy.19.count_ref, s32[1]{0:T(128)} %bitcast.core_ref, ...), custom_call_target="tpu_custom_call" | custom-call | flops 800000000 | bytes 4000000 | tf_op jit(solution)/shard_map/pallas_call | solution.py:274
  5.6 8.8 %collective-permute-start = (bf16[208,16,128]{2,1,0:T(8,128)(2,1)S(1)}, bf16[208,16,128]{2,1,0:T(8,128)(2,1)}, u32[]{:S(2)}, u32[]{:S(2)}) collective-permute-start(bf16[208,16,128]{2,1,0:T(8,128)(2,1)S(1)} %get-tuple-element.32), channel_id=1, source_target_pairs={{0,16},{16,0},{1,17},{17,1},{2,18},{18,2},{3,19},{19,3},{4,20},{20... | collective-permute-start | bytes 2555912 | tf_op jit(solution)/shard_map/ppermute | solution.py:351
  14.4 0.0 copy-done
  14.4 0.1 reshape.36
  14.5 0.1 pad.16.clone
  14.6 0.0 copy-done.1
  14.6 0.1 maximum_maximum_fusion
  14.7 1.1 %shard_map.119 = (bf16[208,16,128]{2,1,0:T(8,128)(2,1)S(1)}, bf16[320,320]{1,0:T(8,128)(2,1)S(1)}) custom-call(s32[1]{0:T(128)} %bitcast.core_ref, bf16[320,640]{1,0:T(8,128)(2,1)S(1)} %get-tuple-element.27.natural, bf16[320,1280]{1,0:T(8,128)(2,1)S(1)} %get-tuple-element.28.g_ref, f32[1,1280]{1,0:T(1,128)S(1)} %get-tuple-element.29.bias_ref), custom_call_target="tpu_custom_call" | custom-call | flops 300000000 | bytes 4000000 | tf_op jit(solution)/shard_map/pallas_call | solution.py:294
  15.9 0.6 collective-permute-done
  16.5 1.4 %reduce_sum.34 = bf16[208,16,128]{2,1,0:T(8,128)(2,1)S(1)} add(bf16[208,16,128]{2,1,0:T(8,128)(2,1)S(1)} %get-tuple-element.31, bf16[208,16,128]{2,1,0:T(8,128)(2,1)} %collective-permute-done) | non-fusion elementwise | flops 425984 | bytes 2555904 | tf_op jit(solution)/shard_map/reduce_sum | solution.py:355
  17.9 17.2 %all_to_all.15 = bf16[16,13,16,128]{3,2,1,0:T(8,128)(2,1)S(1)} all-to-all(bf16[16,13,16,128]{3,2,1,0:T(8,128)(2,1)S(1)} %bitcast.17), channel_id=1, replica_groups=mesh['z'=16,'c'=2,'y'=4,'x'=4] {'y','x'}, dimensions={0} | all-to-all | bytes 1703936 | tf_op jit(solution)/shard_map/all_to_all | solution.py:347
  35.1 0.1 reduce_sum.35
  35.3 25.2 %all_to_all.16 = bf16[16,26,128]{2,1,0:T(8,128)(2,1)S(1)} all-to-all(bf16[16,26,128]{2,1,0:T(8,128)(2,1)S(1)} %copy.16), channel_id=1, replica_groups=mesh['z'=16,'c'=2,'y'=4,'x'=4] {'z'}, dimensions={0} | all-to-all | bytes 212992 | tf_op jit(solution)/shard_map/all_to_all | solution.py:347
  60.6 0.1 broadcast_in_dim.28
  60.7 15.3 %all_to_all.17.near_ref = bf16[16,14,16,128]{3,2,1,0:T(8,128)(2,1)S(1)} all-to-all(bf16[16,14,16,128]{3,2,1,0:T(8,128)(2,1)S(1)} %broadcast_in_dim.28), channel_id=1, replica_groups=mesh['z'=16,'c'=2,'y'=4,'x'=4] {'y','x'}, dimensions={0} | all-to-all | bytes 1835008 | tf_op jit(solution)/shard_map/all_to_all | solution.py:347
  76.1 6.4 %collective-permute-start.1 = (bf16[16,14,16,128]{3,2,1,0:T(8,128)(2,1)S(1)}, bf16[16,14,16,128]{3,2,1,0:T(8,128)(2,1)S(1)}, u32[]{:S(2)}, u32[]{:S(2)}) collective-permute-start(bf16[16,14,16,128]{3,2,1,0:T(8,128)(2,1)S(1)} %all_to_all.17.near_ref), channel_id=1, source_target_pairs={{0,16},{16,0},{1,17},{17,1},{2,18},{18,2},{3,19},{19,3},{4,20},{20... | collective-permute-start | bytes 2752520 | tf_op jit(solution)/shard_map/ppermute | solution.py:351
  82.5 1.8 %shard_map.120 = (bf16[5,64,640]{2,1,0:T(8,128)(2,1)S(1)}, bf16[5,64,640]{2,1,0:T(8,128)(2,1)S(1)}, bf16[5,64,640]{2,1,0:T(8,128)(2,1)S(1)}, bf16[320,1280]{1,0:...) custom-call(s32[1]{0:T(128)} %bitcast.core_ref, ...), custom_call_target="tpu_custom_call" | custom-call | flops 600000000 | bytes 4000000 | tf_op jit(solution)/shard_map/pallas_call | solution.py:309
  84.3 0.5 fusion
  84.9 0.0 collective-permute-done.1.far_ref
  84.9 5.9 %shard_map.121 = (bf16[5,64,1280]{2,1,0:T(8,128)(2,1)}, bf16[5,64,640]{2,1,0:T(8,128)(2,1)}, bf16[5,64,640]{2,1,0:T(8,128)(2,1)}, bf16[5,64,640]{2,1,0:T(8,128)(2,1)}) custom-call(s32[1]{0:T(128)S(6)} %copy.19.count_ref, s32[1]{0:T(128)} %bitcast.core_ref, bf16[5,64,640]{2,1,0:T(8,128)(2,1)S(1)} %get-tuple-element.35.q_ref, ...), custom_call_target="tpu_custom_call" | custom-call | flops 1200000000 | bytes 4000000 | tf_op jit(solution)/shard_map/pallas_call | solution.py:332
  (12 shorter events, 0.2 us)
Async XLA Ops:
  0.6 13.7 %copy-start = (bf16[20,1280]{1,0:T(8,128)(2,1)S(1)}, bf16[20,1280]{1,0:T(8,128)(2,1)}, u32[]{:S(2)}) copy-start(bf16[20,1280]{1,0:T(8,128)(2,1)} %param.11) | copy-start | bytes 153604
  0.6 13.9 %copy-start.1 = (bf16[40]{0:T(256)(128)(2,1)S(1)}, bf16[40]{0:T(256)(128)(2,1)}, u32[]{:S(2)}) copy-start(bf16[40]{0:T(256)(128)(2,1)} %param.12) | copy-start | bytes 244
  5.6 10.9 %collective-permute-start = (bf16[208,16,128]{2,1,0:T(8,128)(2,1)S(1)}, bf16[208,16,128]{2,1,0:T(8,128)(2,1)}, u32[]{:S(2)}, u32[]{:S(2)}) collective-permute-start(bf16[208,16,128]{2,1,0:T(8,128)(2,1)S(1)} %get-tuple-element.32), channel_id=1, source_target_pairs={{0,16},{16,0},{1,17},{17,1},{2,18},{18,2},{3,19},{19,3},{4,20},{20... | collective-permute-start | bytes 2555912 | tf_op jit(solution)/shard_map/ppermute | solution.py:351
  76.1 8.8 %collective-permute-start.1 = (bf16[16,14,16,128]{3,2,1,0:T(8,128)(2,1)S(1)}, bf16[16,14,16,128]{3,2,1,0:T(8,128)(2,1)S(1)}, u32[]{:S(2)}, u32[]{:S(2)}) collective-permute-start(bf16[16,14,16,128]{3,2,1,0:T(8,128)(2,1)S(1)} %all_to_all.17.near_ref), channel_id=1, source_target_pairs={{0,16},{16,0},{1,17},{17,1},{2,18},{18,2},{3,19},{19,3},{4,20},{20... | collective-permute-start | bytes 2752520 | tf_op jit(solution)/shard_map/ppermute | solution.py:351
